TPU v7x, 128 devices: a whole 4x4x4 slice. The times are simulated.
128 devices in a mesh: wide: 32 (over z, y, core), narrow: 4 (over x).
Axes of the slice: x: 4, y: 4, z: 4, core: 2. Of those that a mesh axis runs over, the one named last changes fastest.
Arguments:
- psi_val: bfloat16 [128, 32768], replicated, may hold values from -6 to 6
- psi_cond: bfloat16 [32, 32768], replicated, may hold values from -6 to 6
- energy_val: float32 [128], replicated, may hold values from -8 to -1
- energy_cond: float32 [32], replicated, may hold values from 0.5 to 6
- pair_table: int32 [2048, 2], P(('wide', 'narrow')), may hold values from 0 to 127, as said below
- sphere_map: int32 [8192], replicated, may hold values from 0 to 32767, as said below
Outputs:
- chi_real: float32 [8192, 8192], P('wide', 'narrow')
- chi_imag: float32 [8192, 8192], P('wide', 'narrow')
Inputs may be any that keep to these rules, and one draw needn't show every extreme that they name: `pair_table`: every row is a distinct pair; the column-1 entries are below 32; the valence bands present are 64 distinct bands, each paired with all 32 conduction bands, and band 128 - 1 is among them. `sphere_map`: distinct grid indices of the 8192 G-vectors with the smallest lengths (wrapped frequencies), in no particular order; ties among equal lengths are drawn.
All inputs are finite; a program needn't handle non-finite values.
Results may differ from a plain program's by a relative error of at most 0.004.
Values may be sent and summed in bfloat16 or wider, within the bound.
A program may use at most 128 MiB of HBM per device.

v0:
```python
import math

import jax
import jax.numpy as jnp
from jax import lax
from jax.sharding import PartitionSpec as P

FS = 32
NC = 32
VB = 64


def spectrum_rows(density, sphere_map):
    grid_side = FS
    plane_size = grid_side * grid_side
    local_pairs = density.shape[0]
    plane_index = jnp.arange(plane_size, dtype=jnp.int32)
    index_y = plane_index // grid_side
    index_z = plane_index % grid_side
    phases = (index_y[:, None] * index_y[None, :] + index_z[:, None] * index_z[None, :]) % grid_side
    angles = phases.astype(jnp.float32) * (2.0 * math.pi / grid_side)
    plane_table = jnp.concatenate([jnp.cos(angles), -jnp.sin(angles)], axis=1)
    line_index = jnp.arange(grid_side, dtype=jnp.int32)
    line_angles = (line_index[:, None] * line_index[None, :] % grid_side).astype(jnp.float32) * (
        2.0 * math.pi / grid_side
    )
    cos_line = jnp.cos(line_angles)
    sin_line = jnp.sin(line_angles)
    precise = lax.Precision.HIGH
    shaped = density.reshape(local_pairs * grid_side, plane_size)
    plane_both = jnp.dot(shaped, plane_table, precision=precise, preferred_element_type=jnp.float32)
    plane_both = plane_both.reshape(local_pairs, grid_side, 2 * plane_size)
    cos_both = jnp.einsum("kx,pxq->kqp", cos_line, plane_both, precision=precise)
    sin_both = jnp.einsum("kx,pxq->kqp", sin_line, plane_both, precision=precise)
    full_real = cos_both[:, :plane_size] + sin_both[:, plane_size:]
    full_imag = cos_both[:, plane_size:] - sin_both[:, :plane_size]
    norm_scale = float(grid_side) ** (-1.5)
    stacked = (
        jnp.concatenate(
            [full_real.reshape(-1, local_pairs), full_imag.reshape(-1, local_pairs)], axis=1
        )
        * norm_scale
    )
    picked = jnp.take(stacked, sphere_map, axis=0)
    return picked.T.reshape(2, local_pairs, -1)


def contract(left_block, right_block):
    return lax.dot_general(
        left_block, right_block, (((0, 1), (0, 1)), ((), ())), preferred_element_type=jnp.float32
    )


def on_device(psi_val, psi_cond, energy_val, energy_cond, pair_table, sphere_map):
    val_index = pair_table[:, 0]
    cond_index = pair_table[:, 1]
    left_wave = jnp.take(psi_val, val_index, axis=0).astype(jnp.float32)
    right_wave = jnp.take(psi_cond, cond_index, axis=0).astype(jnp.float32)
    sphere_parts = spectrum_rows(left_wave * right_wave, sphere_map)
    val_hit = val_index[:, None] == jnp.arange(energy_val.shape[0], dtype=jnp.int32)[None, :]
    cond_hit = cond_index[:, None] == jnp.arange(energy_cond.shape[0], dtype=jnp.int32)[None, :]
    val_energy = jnp.sum(jnp.where(val_hit, energy_val[None, :], 0.0), axis=1)
    cond_energy = jnp.sum(jnp.where(cond_hit, energy_cond[None, :], 0.0), axis=1)
    weight = 2.0 / ((val_energy - cond_energy) * math.sqrt(VB * NC))
    plain = sphere_parts.astype(jnp.bfloat16)
    weighted = (weight[None, :, None] * sphere_parts).astype(jnp.bfloat16)
    grown = lax.all_gather(weighted, "narrow", axis=1, tiled=True)
    row_real = lax.all_to_all(grown, "wide", split_axis=2, concat_axis=1, tiled=True)
    row_imag = jnp.stack([row_real[1], -row_real[0]])
    column_parts = lax.all_to_all(plain, "narrow", split_axis=2, concat_axis=1, tiled=True)
    shard_piece = lax.all_gather(column_parts, "wide", axis=1, tiled=True)
    chi_real = contract(row_real, shard_piece)
    chi_imag = contract(row_imag, shard_piece)
    return (chi_real, chi_imag)


def solution(mesh):
    placed = (P(), P(), P(), P(), P(("wide", "narrow"), None), P())
    return jax.shard_map(
        on_device,
        mesh=mesh,
        in_specs=placed,
        out_specs=(P("wide", "narrow"), P("wide", "narrow")),
        check_vma=False,
    )
```

profile of v0, /device:TPU:1, one launch (start us, length us, event | category | flops | bytes accessed | tf_op | source)
XLA Modules:
  0.0 290.6 jit_solution(4690895403465103417)
XLA Ops:
  10.4 1.2 gather_fusion.1
  12.2 6.6 %gather_fusion = bf16[16,32768]{1,0:T(8,128)(2,1)S(1)} fusion(bf16[128,32768]{1,0:T(8,128)(2,1)} %param.6, s32[1024]{0:T(1024)S(1)} %get-tuple-element.17), kind=kCustom, calls=%fused_computation | custom fusion | bytes 2097216 | tf_op jit(solution)/shard_map/jit(_take)/gather | solution.py:57
  19.8 17.7 %fusion.6 = (f32[1024,1024]{1,0:T(8,128)S(1)}, f32[1024,1024]{1,0:T(8,128)S(1)}) fusion(s32[1024]{0:T(1024)S(1)} %get-tuple-element.14, s32[1024]{0:T(1024)S(1)} %get-tuple-element.15), kind=kLoop, calls=%fused_computation.20 | loop fusion | flops 17825792 | bytes 8396800 | tf_op jit(solution)/shard_map/cos | solution.py:22
  37.5 7.5 %fusion = f32[16,32,2048]{2,1,0:T(8,128)S(1)} fusion(f32[1024,1024]{1,0:T(8,128)S(1)} %get-tuple-element.7, f32[1024,1024]{1,0:T(8,128)S(1)} %get-tuple-element.6, bf16[16,32,1024]{2,1,0:T(8,128)(2,1)S(1)} %bitcast_select_fusion, bf16[16,32,1024]{2,1,0:T(8,128)(2,1)S(1)} %bitcast_select_fusion.1), kind=kOutput, calls=%fused_computation.4 | convolution fusion | flops 6446120960 | bytes 14680064 | tf_op jit(solution)/shard_map/dot_general | solution.py:31
  45.0 2.7 convolution_bitcast_fusion
  47.7 2.7 convolution_bitcast_fusion.1
  50.3 1.1 slice_add_fusion
  51.5 1.4 copy.65
  52.9 1.2 copy.66
  54.1 2.3 maximum_multiply_fusion
  56.4 10.3 %copy.46 = f32[32768,32]{1,0:T(8,128)} copy(f32[32768,32]{0,1:T(8,128)} %maximum_multiply_fusion) | data formatting | bytes 8388608 | tf_op jit(solution)/shard_map/mul | solution.py:39
  66.8 33.7 %gather_fusion.2 = f32[8192,32]{1,0:T(8,128)} fusion(f32[32768,32]{1,0:T(8,128)} %copy.46, s32[8192]{0:T(1024)S(1)} %fusion.13), kind=kCustom, calls=%fused_computation.2 | custom fusion | bytes 2129920 | tf_op jit(solution)/shard_map/jit(_take)/gather | solution.py:44
  100.4 7.5 %select_bitcast_fusion = f32[32,8192]{0,1:T(8,128)} fusion(f32[8192,32]{1,0:T(8,128)} %gather_fusion.2, pred[8192]{0:T(1024)(128)(4,1)S(1)} %compare_and_fusion), kind=kLoop, calls=%fused_computation.14 | loop fusion | flops 262144 | bytes 2105344 | tf_op jit(solution)/shard_map/jit(_take)/select_n | solution.py:44
  107.9 2.8 copy.47
  112.2 6.7 %copy.51 = bf16[2,16,8192]{1,0,2:T(2,128)(2,1)} copy(bf16[2,16,8192]{2,1,0:T(8,128)(2,1)S(1)} %convert_element_type.31) | data formatting | bytes 1048576 | tf_op jit(solution)/shard_map/convert_element_type | solution.py:65
  118.9 5.8 %reshape.147 = bf16[4,2,32768]{2,1,0:T(2,128)(2,1)S(1)} reshape(bf16[8192,2,16]{2,1,0:T(2,128)(2,1)} %bitcast.67) | data formatting | bytes 1048576
  124.6 19.5 %all_to_all.36 = bf16[4,2,32768]{2,1,0:T(2,128)(2,1)S(1)} all-to-all(bf16[4,2,32768]{2,1,0:T(2,128)(2,1)S(1)} %reshape.147), channel_id=1, replica_groups=mesh['wide'=32,'narrow'=4] {'narrow'}, dimensions={0} | all-to-all | bytes 1048576 | tf_op jit(solution)/shard_map/all_to_all | solution.py:70
  144.1 4.1 %reshape.148 = bf16[8192,2,16]{2,1,0:T(2,128)(2,1)} reshape(bf16[4,2,32768]{2,1,0:T(2,128)(2,1)S(1)} %all_to_all.36) | data formatting | bytes 1048576
  148.2 9.7 %copy.62 = bf16[2,16,4,2048]{3,2,1,0:T(4,128)(2,1)S(1)} copy(bf16[2,16,4,2048]{1,0,3,2:T(2,128)(2,1)} %bitcast.68) | data formatting | bytes 1048576 | tf_op jit(solution)/shard_map/all_to_all | solution.py:70
  159.1 9.5 %copy.48 = bf16[2,64,8192]{1,0,2:T(2,128)(2,1)} copy(bf16[2,64,8192]{2,1,0:T(8,128)(2,1)} %all-gather.3.cloned.1.call-done) | data formatting | bytes 4194304 | tf_op jit(solution)/shard_map/all_gather | solution.py:67
  168.6 9.1 %reshape.145 = bf16[32,2,16384]{2,1,0:T(2,128)(2,1)S(1)} reshape(bf16[8192,2,64]{2,1,0:T(2,128)(2,1)} %bitcast.69) | data formatting | bytes 4194304
  177.7 53.8 %all_to_all.37 = bf16[32,2,16384]{2,1,0:T(2,128)(2,1)} all-to-all(bf16[32,2,16384]{2,1,0:T(2,128)(2,1)S(1)} %reshape.145), channel_id=1, replica_groups=mesh['wide'=32,'narrow'=4] {'wide'}, dimensions={0} | all-to-all | bytes 4194304 | tf_op jit(solution)/shard_map/all_to_all | solution.py:68
  231.5 9.7 %reshape.146 = bf16[8192,2,64]{2,1,0:T(2,128)(2,1)} reshape(bf16[32,2,16384]{2,1,0:T(2,128)(2,1)} %all_to_all.37) | data formatting | bytes 4194304
  241.3 9.0 %copy.61 = bf16[2,64,32,256]{3,1,2,0:T(8,128)(2,1)S(1)} copy(bf16[2,64,32,256]{1,0,3,2:T(2,128)(2,1)} %bitcast.65) | data formatting | bytes 4194304 | tf_op jit(solution)/shard_map/all_to_all | solution.py:68
  250.3 7.3 %copy.60 = bf16[2,64,32,256]{3,2,1,0:T(8,128)(2,1)} copy(bf16[2,64,32,256]{1,0,3,2:T(2,128)(2,1)} %bitcast.66) | data formatting | bytes 4194304 | tf_op jit(solution)/shard_map/all_to_all | solution.py:68
  257.7 2.6 fusion.45
  260.9 1.4 copy.57
  262.3 1.8 copy.56
  264.2 1.4 copy.58
  265.6 9.6 %convolution_bitcast_fusion.3 = f32[256,2048]{1,0:T(8,128)} fusion(bf16[2,2048,256]{2,1,0:T(8,128)(2,1)S(1)} %bitcast.70, bf16[2,2048,2048]{2,1,0:T(8,128)(2,1)} %all-gather.5.cloned.1.call-done), kind=kOutput, calls=%fused_computation.19 | convolution fusion | flops 4294967296 | bytes 20971520 | tf_op jit(solution)/shard_map/dot_general | solution.py:49
  275.2 1.7 copy-done.2
  277.4 6.0 %convolution_bitcast_fusion.2 = f32[256,2048]{1,0:T(8,128)} fusion(bf16[2,2048,2048]{2,1,0:T(8,128)(2,1)S(1)} %copy-done.2, bf16[1,2048,256]{1,2,0:T(8,128)(2,1)S(1)} %copy-done.4, bf16[1,2048,256]{1,2,0:T(8,128)(2,1)S(1)} %copy-done.3), kind=kOutput, calls=%fused_computation.18 | convolution fusion | flops 4296015872 | bytes 20971520 | tf_op jit(solution)/shard_map/dot_general | solution.py:49
  (36 shorter events, 8.5 us)
Async XLA Ops:
  7.2 3.2 %copy-start = (bf16[32,32768]{1,0:T(8,128)(2,1)S(1)}, bf16[32,32768]{1,0:T(8,128)(2,1)}, u32[]{:S(2)}) copy-start(bf16[32,32768]{1,0:T(8,128)(2,1)} %param.7) | copy-start | bytes 6291460
  7.2 151.9 %all-gather.3.cloned.1.call-start = ((), (), s32[]{:S(2)}) async-start(), calls=%async_computation.2 | async-start | bytes 2621440 | tf_op jit(solution)/shard_map/all_gather | solution.py:67
  107.9 2.8 copy-start.5
  107.9 3.0 %copy-start.6 = (f32[128]{0:T(128)S(1)}, f32[128]{0:T(128)}, u32[]{:S(2)}) copy-start(f32[128]{0:T(128)} %param.8) | copy-start | bytes 1540
  112.1 153.5 %all-gather.5.cloned.1.call-start = ((), (), s32[]{:S(2)}) async-start(), calls=%async_computation.3 | async-start | bytes 17301504 | tf_op jit(solution)/shard_map/all_gather | solution.py:71
  265.6 11.3 %copy-start.2 = (bf16[2,2048,2048]{2,1,0:T(8,128)(2,1)S(1)}, bf16[2,2048,2048]{2,1,0:T(8,128)(2,1)}, u32[]{:S(2)}) copy-start(bf16[2,2048,2048]{2,1,0:T(8,128)(2,1)} %all-gather.5.cloned.1.call-done) | copy-start | bytes 50331652
  265.6 11.5 %copy-start.3 = (bf16[1,2048,256]{1,2,0:T(8,128)(2,1)S(1)}, bf16[1,2048,256]{1,2,0:T(8,128)(2,1)}, u32[]{:S(2)}) copy-start(bf16[1,2048,256]{1,2,0:T(8,128)(2,1)} %copy.57) | copy-start | bytes 3145732
  265.6 11.8 %copy-start.4 = (bf16[1,2048,256]{1,2,0:T(8,128)(2,1)S(1)}, bf16[1,2048,256]{1,2,0:T(8,128)(2,1)}, u32[]{:S(2)}) copy-start(bf16[1,2048,256]{1,2,0:T(8,128)(2,1)} %copy.58) | copy-start | bytes 3145732
  277.4 6.0 %copy-start.1 = (bf16[32,32768]{1,0:T(8,128)(2,1)S(1)}, bf16[32,32768]{1,0:T(8,128)(2,1)}, u32[]{:S(2)}) copy-start(bf16[32,32768]{1,0:T(8,128)(2,1)} %param.7) | copy-start | bytes 6291460
Sparse Core Ops, SparseCore 0:
  112.2 39.6 all-gather.2
  159.2 91.5 all-gather.4
where the time goes:
time: 296 us; the launch traced here: 291 us
  local copies, waits for them, and re-layouts  138 us (47%)
  blocking collectives  73.3 us (25%)
  other arithmetic  36.2 us (12%)
  matrix products  28.4 us (10%)
  between operations  14.7 us (5%)
    all_to_all x1, blocking collectives, on_device(): lax.all_to_all(grown, 'wide', split_axis=2, concat_axis=1, tiled=True)  53.8 us
    unnamed x22, local copies, waits for them, and re-layouts  34.8 us
    gather x1, local copies, waits for them, and re-layouts, spectrum_rows(): picked = jnp.take(stacked, sphere_map, axis=0)  33.7 us
    all_to_all x1, blocking collectives, on_device(): lax.all_to_all(plain, 'narrow', split_axis=2, concat_axis=1, tiled=True)  19.5 us
    cos x1, other arithmetic, spectrum_rows(): plane_table = jnp.concatenate([jnp.cos(angles), -jnp.sin(angles)], axis=1)  17.7 us
    all_to_all x2, local copies, waits for them, and re-layouts, on_device(): lax.all_to_all(grown, 'wide', split_axis=2, concat_axis=1, tiled=True)  16.4 us
    dot_general x2, matrix products, contract(): lax.dot_general(left_block, right_block, (((0, 1), (0, 1)), ((), ())), pr...  15.6 us
    all_to_all x2, local copies, waits for them, and re-layouts, on_device(): lax.all_to_all(plain, 'narrow', split_axis=2, concat_axis=1, tiled=True)  10.8 us
  transfers between devices with their start and end apart: 2, of which 0 were waited for; matrix products, arithmetic and copies ran while one was open for 28% of the time, Pallas kernels for 0%

commit v1 on v0

v1 whole, which is shorter than its diff:
```python
import functools
import math

import jax
import jax.numpy as jnp
import numpy as np
from jax import lax
from jax.experimental import pallas as pl
from jax.experimental.pallas import tpu as pltpu
from jax.sharding import PartitionSpec as P

FS = 32
NC = 32
VB = 64
NG = 8192
PLANE = FS * FS
KX = 13
MESH = pl.DeviceIdType.MESH
BF = jnp.bfloat16
F32 = jnp.float32


def wrapped(index):
    return np.where(index >= FS // 2, index - FS, index)


def half_plane():
    index = np.arange(FS**3)
    length = wrapped(index // PLANE) ** 2 + wrapped(index // FS % FS) ** 2 + wrapped(index % FS) ** 2
    most = np.sort(length)[NG - 1]
    points = [
        (ky, kz)
        for ky in range(-15, 16)
        for kz in range(-15, 16)
        if ky * ky + kz * kz <= most and (ky > 0 or (ky == 0 and kz >= 0))
    ]
    points.sort(key=lambda point: (point[0] ** 2 + point[1] ** 2, point))
    return np.array(points)


POINTS = half_plane()
HALF = 256
TABLE_SCALE = 1.6211
TABLE_GAIN = 1.6245055860070914


def plane_table():
    flat = np.arange(PLANE)
    phase = (flat // FS)[:, None] * POINTS[:, 0][None, :] + (flat % FS)[:, None] * POINTS[:, 1][None, :]
    angle = (phase % FS) * (2.0 * math.pi / FS)
    table = np.zeros((PLANE, 2 * HALF), np.float64)
    table[:, : len(POINTS)] = np.cos(angle)
    table[:, HALF : HALF + len(POINTS)] = np.sin(angle)
    table[np.abs(table) < 1e-9] = 0.0
    return (table * TABLE_SCALE).astype(np.float32)


def plane_labels():
    labels = np.full((2 * HALF, 1), -1, np.int32)
    for row, (ky, kz) in enumerate(POINTS):
        labels[row, 0] = (ky % FS) * FS + kz % FS
        if (ky, kz) != (0, 0):
            labels[HALF + row, 0] = (-ky % FS) * FS + (-kz) % FS
    return labels


def cosine(step):
    return math.cos(2.0 * math.pi * step / FS)


def combine(terms):
    total = None
    for factor, term in terms:
        if abs(factor) < 1e-12:
            continue
        if abs(abs(factor) - 1.0) < 1e-12:
            value = term
            if total is None:
                total = value if factor > 0 else -value
            else:
                total = total + value if factor > 0 else total - value
        else:
            value = term * factor
            total = value if total is None else total + value
    return total


def even_part(values, period, wanted):
    half = period // 2
    stride = FS // period
    out = {}
    odd = [k for k in wanted if k % 2]
    rest = [k for k in wanted if k % 2 == 0]
    if half == 1:
        for k in wanted:
            out[k] = values[0] + values[1] if k % 2 == 0 else values[0] - values[1]
        return out
    quarter = half // 2
    if odd:
        diff = [values[j] - values[half - j] for j in range(quarter)]
        for k in odd:
            out[k] = combine([(cosine(stride * j * k), diff[j]) for j in range(quarter)])
    if rest:
        folded = [values[j] + values[half - j] for j in range(quarter)] + [values[quarter]]
        inner = even_part(folded, half, [k // 2 for k in rest])
        for k in rest:
            out[k] = inner[k // 2]
    return out


def odd_part(values, period, wanted):
    half = period // 2
    stride = FS // period
    out = {}
    odd = [k for k in wanted if k % 2]
    rest = [k for k in wanted if k % 2 == 0]
    quarter = half // 2
    if odd:
        folded = [None] + [values[j] + values[half - j] for j in range(1, quarter)] + [values[quarter]]
        for k in odd:
            out[k] = combine(
                [(math.sin(2.0 * math.pi * stride * j * k / FS), folded[j]) for j in range(1, quarter + 1)]
            )
    if rest:
        live = [k for k in rest if k % half]
        if live:
            diff = [None] + [values[j] - values[half - j] for j in range(1, quarter)]
            inner = odd_part(diff, half, [k // 2 for k in live])
            for k in live:
                out[k] = inner[k // 2]
    return out


def transform_kernel(val_ref, cond_ref, table_ref, label_ref, sphere_ref, out_ref, high, low, waves, picked):
    lanes = 128
    rows = 16

    def x_step(step, carry):
        lane = pl.multiple_of(step * lanes, lanes)
        for part in range(2):
            for block in range(NC // rows):
                density = []
                for x in range(FS):
                    cond = cond_ref[block * rows : (block + 1) * rows, pl.ds(pl.multiple_of(x * PLANE + lane, lanes), lanes)]
                    val = val_ref[part : part + 1, pl.ds(pl.multiple_of(x * PLANE + lane, lanes), lanes)]
                    density.append(cond.astype(F32) * val)
                even = [density[0]] + [density[j] + density[FS - j] for j in range(1, 16)] + [density[16]]
                odd = [None] + [density[j] - density[FS - j] for j in range(1, 16)]
                real = even_part(even, FS, list(range(KX)))
                imag = odd_part(odd, FS, list(range(KX)))
                for k in range(KX):
                    for s, value in ((0, real[k]), (1, imag.get(k))):
                        at = k * 128 + s * 64 + part * NC + block * rows
                        if value is None:
                            value = jnp.zeros((rows, lanes), F32)
                        if s == 1:
                            value = -value
                        top = value.astype(BF)
                        high[at : at + rows, pl.ds(lane, lanes)] = top
                        low[at : at + rows, pl.ds(lane, lanes)] = (value - top.astype(F32)).astype(BF)
        return carry

    lax.fori_loop(0, PLANE // lanes, x_step, 0)

    scale = FS ** (-1.5) / TABLE_GAIN

    def plane_step(k, carry):
        at = pl.multiple_of(k * 128, 128)
        both = jnp.dot(high[pl.ds(at, 128), :], table_ref[...], preferred_element_type=F32)
        both = both + jnp.dot(low[pl.ds(at, 128), :], table_ref[...], preferred_element_type=F32)
        both = both * scale
        re_cos, re_sin = both[:64, :HALF], both[:64, HALF:]
        im_cos, im_sin = both[64:, :HALF], both[64:, HALF:]
        waves[pl.ds(at, 64), :HALF] = (re_cos + im_sin).astype(BF)
        waves[pl.ds(at, 64), HALF:] = (re_cos - im_sin).astype(BF)
        waves[pl.ds(at + 64, 64), :HALF] = (im_cos - re_sin).astype(BF)
        waves[pl.ds(at + 64, 64), HALF:] = (im_cos + re_sin).astype(BF)
        return carry

    lax.fori_loop(0, KX, plane_step, 0)

    width = 256

    def pick_step(tile, carry):
        lane = pl.multiple_of(tile * width, width)
        flat = sphere_ref[:, pl.ds(lane, width)]
        kx = flat // PLANE
        ky = flat // FS % FS
        kz = flat % FS
        mirror = kx >= FS // 2
        ky = jnp.where(mirror, (FS - ky) % FS, ky)
        kz = jnp.where(mirror, (FS - kz) % FS, kz)
        kx = jnp.where(mirror, FS - kx, kx)
        sign = jnp.where(mirror, -1.0, 1.0)
        target = ky * FS + kz
        hit = jnp.where(label_ref[...] == target, 1.0, 0.0).astype(BF)
        picked[...] = jnp.dot(waves[...], hit, preferred_element_type=F32)
        total = picked[0:128, :]
        for k in range(1, KX):
            total = jnp.where(kx == k, picked[k * 128 : (k + 1) * 128, :], total)
        out_ref[0:64, pl.ds(lane, width)] = total[:64].astype(BF)
        out_ref[64:128, pl.ds(lane, width)] = (total[64:] * sign).astype(BF)
        return carry

    lax.fori_loop(0, 2048 // width, pick_step, 0)


def transform(val_rows, psi_cond, sphere_block):
    whole = pl.BlockSpec(memory_space=pltpu.VMEM)
    return pl.pallas_call(
        transform_kernel,
        out_shape=jax.ShapeDtypeStruct((128, 2048), BF),
        in_specs=[whole] * 5,
        out_specs=whole,
        scratch_shapes=[
            pltpu.VMEM((KX * 128, PLANE), BF),
            pltpu.VMEM((KX * 128, PLANE), BF),
            pltpu.VMEM((KX * 128, 2 * HALF), BF),
            pltpu.VMEM((KX * 128, 256), F32),
        ],
        compiler_params=pltpu.CompilerParams(vmem_limit_bytes=40 * 2**20),
        cost_estimate=pl.CostEstimate(flops=10**10, bytes_accessed=4 * 2**20, transcendentals=0),
        name="transform",
    )(
        val_rows,
        psi_cond,
        jnp.asarray(plane_table()).astype(BF),
        jnp.asarray(plane_labels()),
        sphere_block,
    )


ORDER = [
    (0, 0), (3, 0), (1, 0), (0, 3), (0, 1), (2, 0), (3, 3), (3, 1),
    (1, 3), (1, 1), (0, 2), (2, 3), (2, 1), (3, 2), (1, 2), (2, 2),
]
SLOT = {place: slot for slot, place in enumerate(ORDER)}


def gather_kernel(own_ref, weight_ref, real_ref, imag_ref, held, rows, part_sem, swap_sem, row_sem, send_sem):
    wide = lax.axis_index("wide")
    x = lax.axis_index("narrow")
    z, y, core = wide // 8, wide // 2 % 4, wide % 2
    a = jnp.where(core == 0, y, z)
    b = jnp.where(core == 0, z, y)

    def at(da, db, other=0):
        aa, bb = (a + da) % 4, (b + db) % 4
        return jnp.where(core == 0, bb * 8 + aa * 2, aa * 8 + bb * 2 + 1)

    peers = {
        "a+": (at(1, 0), x),
        "a-": (at(3, 0), x),
        "b+": (at(0, 1), x),
        "b-": (at(0, 3), x),
        "swap": (wide + 1 - 2 * core, x),
        "x+": (wide, (x + 1) % 4),
        "x-": (wide, (x + 3) % 4),
    }
    barrier = pltpu.get_barrier_semaphore()
    for peer in peers.values():
        pl.semaphore_signal(barrier, inc=1, device_id=peer, device_id_type=MESH)

    held[0, 0, 0:64, :] = own_ref[0:64, :]
    held[0, 1, 0:64, :] = own_ref[64:128, :]
    pl.semaphore_wait(barrier, len(peers))

    sends = []

    def view(slot, part, which=0):
        if part is None:
            return held.at[slot, :, which * 64 : which * 64 + 64, :]
        return held.at[slot, part, which * 64 : which * 64 + 64, :]

    def push(slot, part, peer, target):
        copy = pltpu.make_async_remote_copy(
            src_ref=view(slot, part),
            dst_ref=view(target, part),
            send_sem=send_sem.at[len(sends)],
            recv_sem=part_sem.at[target, part if part is not None else 0],
            device_id=peers[peer],
            device_id_type=MESH,
        )
        copy.start()
        sends.append(copy)

    def arrived(slot, part):
        pltpu.make_async_remote_copy(
            src_ref=view(slot, part),
            dst_ref=view(slot, part),
            send_sem=send_sem.at[0],
            recv_sem=part_sem.at[slot, part if part is not None else 0],
            device_id=peers["a+"],
            device_id_type=MESH,
        ).wait_recv()

    def swap_copy(slot, index):
        return pltpu.make_async_remote_copy(
            src_ref=view(slot, None, 0),
            dst_ref=view(slot, None, 1),
            send_sem=send_sem.at[index],
            recv_sem=swap_sem.at[slot],
            device_id=peers["swap"],
            device_id_type=MESH,
        )

    def own_event(slot):
        da, db = ORDER[slot]
        if slot and (da == 2 and db == 0 or db == 2):
            arrived(slot, 0)
            arrived(slot, 1)
        elif slot:
            arrived(slot, None)
        if db == 0:
            if da == 0:
                push(slot, None, "a+", SLOT[3, 0])
                push(slot, None, "a-", SLOT[1, 0])
            elif da == 3:
                push(slot, 0, "a+", SLOT[2, 0])
            elif da == 1:
                push(slot, 1, "a-", SLOT[2, 0])
            push(slot, None, "b+", SLOT[da, 3])
            push(slot, None, "b-", SLOT[da, 1])
        elif db == 3:
            push(slot, 0, "b+", SLOT[da, 2])
        elif db == 1:
            push(slot, 1, "b-", SLOT[da, 2])
        copy = swap_copy(slot, len(sends))
        copy.start()
        sends.append(copy)

    column = pl.multiple_of((y * 2 + core) * 256, 256)
    hops = ((x - z) % 4, (z - x) % 4)

    def row_copy(slot, which):
        return pltpu.make_async_remote_copy(
            src_ref=rows.at[slot, :, which * 64 : which * 64 + 64, :],
            dst_ref=rows.at[slot, :, which * 64 : which * 64 + 64, :],
            send_sem=row_sem.at[1, slot, which],
            recv_sem=row_sem.at[0, slot, which],
            device_id=peers["x+" if which == 0 else "x-"],
            device_id_type=MESH,
        )

    def row_event(slot, which, hop):
        @pl.when(hops[which] == hop)
        def _():
            if hop == 0:
                rows[slot, :, which * 64 : which * 64 + 64, :] = held[
                    slot, :, which * 64 : which * 64 + 64, pl.ds(column, 256)
                ]
            else:
                row_copy(slot, which).wait_recv()
            if hop < 3:
                row_copy(slot, which).start()

    width = 512

    def product(slot):
        left = rows[slot].reshape(256, 256).astype(F32).T
        left = left * weight_of(slot)
        left_real = left.astype(BF)
        left_imag = jnp.concatenate([left[:, 128:], -left[:, :128]], axis=1).astype(BF)

        def tile(step, carry):
            lane = pl.multiple_of(step * width, width)
            right = held[slot, :, :, pl.ds(lane, width)].reshape(256, width)
            real = jnp.dot(left_real, right, preferred_element_type=F32)
            imag = jnp.dot(left_imag, right, preferred_element_type=F32)
            if slot == 0:
                real_ref[:, pl.ds(lane, width)] = real
                imag_ref[:, pl.ds(lane, width)] = imag
            else:
                real_ref[:, pl.ds(lane, width)] += real
                imag_ref[:, pl.ds(lane, width)] += imag
            return carry

        lax.fori_loop(0, 2048 // width, tile, 0)

    def weight_of(slot):
        da, db = ORDER[slot]
        first = at(da, db)
        aa, bb = (b + da) % 4, (a + db) % 4
        second = jnp.where(core == 0, aa * 8 + bb * 2 + 1, bb * 8 + aa * 2)
        return weight_ref[first] + weight_ref[second + 32]

    lag = 6
    for event in range(16 + lag):
        if event < 16:
            own_event(event)
        if 0 <= event - 1 < 16:
            pltpu.make_async_remote_copy(
                src_ref=view(event - 1, None, 0),
                dst_ref=view(event - 1, None, 1),
                send_sem=send_sem.at[0],
                recv_sem=swap_sem.at[event - 1],
                device_id=peers["swap"],
                device_id_type=MESH,
            ).wait_recv()
        for which in range(2):
            for hop in range(4):
                slot = event - 1 - hop
                if 0 <= slot < 16:
                    row_event(slot, which, hop)
        if 0 <= event - lag + 1 < 16:
            product(event - lag + 1)

    for copy in sends:
        copy.wait_send()
    for slot in range(16):
        for which in range(2):

            @pl.when(hops[which] < 3)
            def _():
                row_copy(slot, which).wait_send()


def gather_and_multiply(own, weights):
    whole = pl.BlockSpec(memory_space=pltpu.VMEM)
    return pl.pallas_call(
        gather_kernel,
        out_shape=[jax.ShapeDtypeStruct((256, 2048), F32)] * 2,
        in_specs=[whole] * 2,
        out_specs=[whole] * 2,
        scratch_shapes=[
            pltpu.VMEM((16, 2, 128, 2048), BF),
            pltpu.VMEM((16, 2, 128, 256), BF),
            pltpu.SemaphoreType.DMA((16, 2)),
            pltpu.SemaphoreType.DMA((16,)),
            pltpu.SemaphoreType.DMA((2, 16, 2)),
            pltpu.SemaphoreType.DMA((64,)),
        ],
        compiler_params=pltpu.CompilerParams(
            collective_id=0, has_side_effects=True, vmem_limit_bytes=48 * 2**20
        ),
        cost_estimate=pl.CostEstimate(flops=2 * 4096 * 512 * 2048, bytes_accessed=8 * 2**20, transcendentals=0),
        name="gather_and_multiply",
    )(own, weights)


def on_device(psi_val, psi_cond, energy_val, energy_cond, pair_table, sphere_map):
    wide = lax.axis_index("wide")
    bands = jnp.arange(128, dtype=jnp.int32)
    present = jnp.max((pair_table[:, :1] == bands[None, :]).astype(F32), axis=0)
    present = lax.psum(present, ("wide", "narrow")) > 0.5
    rank = jnp.sum(((bands[:, None] < bands[None, :]) & present[:, None]).astype(jnp.int32), axis=0)
    chosen = present[None, :] & (rank[None, :] == jnp.arange(VB, dtype=jnp.int32)[:, None])
    band_of = jnp.sum(jnp.where(chosen, bands[None, :], 0), axis=1)
    energy_of = jnp.sum(jnp.where(chosen, energy_val[None, :], 0.0), axis=1)
    weight = 2.0 / ((energy_of[:, None] - energy_cond[None, :]) * math.sqrt(VB * NC))
    weight = weight.reshape(32, 64)
    blank = jnp.zeros_like(weight)
    first = jnp.concatenate([weight, blank, weight, blank], axis=1)
    second = jnp.concatenate([blank, weight, blank, weight], axis=1)
    weights = jnp.concatenate([first, second], axis=0).reshape(64, 1, 256)
    mine = lax.dynamic_slice(band_of, (2 * wide,), (2,))
    val_rows = jnp.concatenate(
        [lax.dynamic_slice(psi_val, (mine[i], 0), (1, psi_val.shape[1])) for i in range(2)], axis=0
    ).astype(F32)
    sphere_block = lax.dynamic_slice(sphere_map, (lax.axis_index("narrow") * 2048,), (2048,)).reshape(1, 2048)
    own = transform(val_rows, psi_cond, sphere_block)
    chi_real, chi_imag = gather_and_multiply(own, weights)
    return (chi_real, chi_imag)


def solution(mesh):
    placed = (P(), P(), P(), P(), P(("wide", "narrow"), None), P())
    return jax.shard_map(
        on_device,
        mesh=mesh,
        in_specs=placed,
        out_specs=(P("wide", "narrow"), P("wide", "narrow")),
        check_vma=False,
    )
```

time: 296 us -> 179 us (0.60)
  the two profiles are of different devices: /device:TPU:1 before, /device:TPU:32 now
where the time goes in v1:
time: 179 us; the launch traced here: 178 us
  Pallas kernels  95.2 us (53%)
  blocking collectives  65.8 us (37%)
  local copies, waits for them, and re-layouts  11 us (6%)
  between operations  4.62 us (3%)
    pallas_call x1, Pallas kernels, gather_and_multiply(): pl.pallas_call(gather_kernel, out_shape=[jax.ShapeDtypeStruct((256, 2048)...  78.2 us
    psum x1, blocking collectives, on_device(): present = lax.psum(present, ('wide', 'narrow')) > 0.5  65.8 us
    pallas_call x1, Pallas kernels, transform(): pl.pallas_call(transform_kernel, out_shape=jax.ShapeDtypeStruct((128, 204...  17 us
    unnamed x8, local copies, waits for them, and re-layouts  6.4 us

profile of v1, /device:TPU:32, one launch (start us, length us, event | category | flops | bytes accessed | tf_op | source)
XLA Modules:
  0.0 178.1 jit_solution(17216355023059198530)
XLA Ops:
  0.6 0.7 slice_bitcast_fusion
  1.3 0.1 convert_reduce_fusion.1
  1.4 65.8 %psum.7 = f32[128]{0:T(128)S(1)} all-reduce(f32[128]{0:T(128)S(1)} %convert_reduce_fusion.1), channel_id=1, replica_groups=mesh['wide'=32,'narrow'=4] {'wide','narrow'}, use_global_device_ids=true, to_apply=%region_1.0 | all-reduce | flops 128 | bytes 1024 | tf_op jit(solution)/shard_map/psum | solution.py:445
  67.2 0.1 convert_reduce_fusion
  67.3 0.8 select_reduce_fusion
  68.1 0.1 select_reduce_fusion.1
  68.2 0.1 dynamic_slice.12
  68.3 0.6 fusion.2
  72.8 0.7 sub.25
  73.4 0.1 sub.26
  73.5 0.7 dynamic_slice.15
  74.2 0.1 sub.22
  74.3 0.1 sub.23
  74.4 0.1 sub.24
  74.5 0.1 maximum_maximum_fusion
  74.7 1.5 constant_dynamic-slice_fusion.1
  76.2 0.3 maximum_convert_fusion.val_ref
  76.5 0.0 copy-start
  76.5 1.6 copy-done
  78.1 0.0 copy-start.1
  78.1 1.2 copy-done.1
  79.3 0.0 copy-start.2
  79.3 0.9 copy-done.2
  80.3 17.0 %transform.1.own_ref = bf16[128,2048]{1,0:T(8,128)(2,1)S(1)} custom-call(f32[2,32768]{1,0:T(2,128)S(1)} %maximum_convert_fusion.val_ref, bf16[32,32768]{1,0:T(8,128)(2,1)S(1)} %copy-done, bf16[1024,512]{1,0:T(8,128)(2,1)S(1)} %copy-done.1, s32[512,1]{1,0:T(8,128)S(1)} %copy-done.2, s32[1,2048]{1,0:T(1,128)S(1)} %bitcast.5), custom_call_target="tpu_custom_call" | custom-call | flops 10000000000 | bytes 4194304 | tf_op jit(solution)/shard_map/transform/pallas_call | solution.py:210
  97.3 78.2 %gather_and_multiply.1 = (f32[256,2048]{1,0:T(8,128)S(1)}, f32[256,2048]{1,0:T(8,128)S(1)}) custom-call(bf16[128,2048]{1,0:T(8,128)(2,1)S(1)} %transform.1.own_ref, f32[64,1,256]{2,1,0:T(1,128)S(1)} %reshape.22.weight_ref), custom_call_target="tpu_custom_call" | custom-call | flops 8589934592 | bytes 8388608 | tf_op jit(solution)/shard_map/gather_and_multiply/pallas_call | solution.py:420
  175.5 1.3 copy.12
  176.8 1.3 copy.13
  (4 shorter events, 0.1 us)
Async XLA Ops:
  76.5 1.6 copy-start
  78.1 1.2 copy-start.1
  79.3 0.9 copy-start.2

commit v2 on v1

--- a/solution.py
+++ b/solution.py
@@ -1,4 +1,3 @@
-import functools
 import math
 
 import jax
@@ -131,7 +130,60 @@
     return out
 
 
-def transform_kernel(val_ref, cond_ref, table_ref, label_ref, sphere_ref, out_ref, high, low, waves, picked):
+def exchange(mask, groups, own, got, out_sem, in_sem):
+    own[0] = mask
+    done, count = [], 0
+    for step, group in enumerate(groups):
+        copies = []
+        for peer in group:
+            copy = pltpu.make_async_remote_copy(
+                src_ref=own.at[step],
+                dst_ref=got.at[count],
+                send_sem=out_sem.at[count],
+                recv_sem=in_sem.at[count],
+                device_id=peer,
+                device_id_type=MESH,
+            )
+            copy.start()
+            copies.append((copy, count))
+            count += 1
+        total = own[step]
+        for copy, at in copies:
+            copy.wait_recv()
+            total = jnp.maximum(total, got[at])
+        own[step + 1] = total
+        done += copies
+    for copy, _ in done:
+        copy.wait_send()
+    return own[len(groups)][0:1, :]
+
+
+def deal(present, wide, val_energy, cond_energy, weight_ref):
+    band = lax.broadcasted_iota(jnp.int32, (128, 128), 0)
+    other = lax.broadcasted_iota(jnp.int32, (128, 128), 1)
+    rank = jnp.sum(jnp.where(other < band, present, 0), axis=1, keepdims=True)
+    across = jnp.sum(jnp.where(other == band, rank, 0), axis=0, keepdims=True)
+    across = jnp.where(present > 0, across, -1)
+    device = lax.broadcasted_iota(jnp.int32, (32, 128), 0)
+    energy = [jnp.sum(jnp.where(across == 2 * device + i, val_energy, 0.0), axis=1, keepdims=True) for i in range(2)]
+    lane = lax.broadcasted_iota(jnp.int32, (32, 256), 1)
+    cond = jnp.concatenate([cond_energy] * 8, axis=1)
+    gap = jnp.where(lane // NC % 2 == 0, energy[0], energy[1]) - cond
+    weight_ref[...] = 2.0 / (gap * math.sqrt(VB * NC))
+    row = lax.broadcasted_iota(jnp.int32, (8, 128), 0)
+    return jnp.where((across == 2 * wide + row) & (row < 2), 1.0, 0.0).astype(BF)
+
+
+def pick_rows(psi_ref, chosen, row_ref):
+    def step(x, carry):
+        lane = pl.multiple_of(x * PLANE, PLANE)
+        row_ref[:, pl.ds(lane, PLANE)] = jnp.dot(chosen, psi_ref[:, pl.ds(lane, PLANE)], preferred_element_type=F32)
+        return carry
+
+    lax.fori_loop(0, FS, step, 0)
+
+
+def transform(val_ref, cond_ref, table_ref, label_ref, sphere_ref, first_column, store, high, low, waves, picked):
     lanes = 128
     rows = 16
 
@@ -183,7 +235,7 @@
 
     def pick_step(tile, carry):
         lane = pl.multiple_of(tile * width, width)
-        flat = sphere_ref[:, pl.ds(lane, width)]
+        flat = sphere_ref[:, pl.ds(pl.multiple_of(first_column + lane, width), width)]
         kx = flat // PLANE
         ky = flat // FS % FS
         kz = flat % FS
@@ -198,36 +250,10 @@
         total = picked[0:128, :]
         for k in range(1, KX):
             total = jnp.where(kx == k, picked[k * 128 : (k + 1) * 128, :], total)
-        out_ref[0:64, pl.ds(lane, width)] = total[:64].astype(BF)
-        out_ref[64:128, pl.ds(lane, width)] = (total[64:] * sign).astype(BF)
+        store(lane, width, total[:64].astype(BF), (total[64:] * sign).astype(BF))
         return carry
 
     lax.fori_loop(0, 2048 // width, pick_step, 0)
-
-
-def transform(val_rows, psi_cond, sphere_block):
-    whole = pl.BlockSpec(memory_space=pltpu.VMEM)
-    return pl.pallas_call(
-        transform_kernel,
-        out_shape=jax.ShapeDtypeStruct((128, 2048), BF),
-        in_specs=[whole] * 5,
-        out_specs=whole,
-        scratch_shapes=[
-            pltpu.VMEM((KX * 128, PLANE), BF),
-            pltpu.VMEM((KX * 128, PLANE), BF),
-            pltpu.VMEM((KX * 128, 2 * HALF), BF),
-            pltpu.VMEM((KX * 128, 256), F32),
-        ],
-        compiler_params=pltpu.CompilerParams(vmem_limit_bytes=40 * 2**20),
-        cost_estimate=pl.CostEstimate(flops=10**10, bytes_accessed=4 * 2**20, transcendentals=0),
-        name="transform",
-    )(
-        val_rows,
-        psi_cond,
-        jnp.asarray(plane_table()).astype(BF),
-        jnp.asarray(plane_labels()),
-        sphere_block,
-    )
 
 
 ORDER = [
@@ -237,7 +263,11 @@
 SLOT = {place: slot for slot, place in enumerate(ORDER)}
 
 
-def gather_kernel(own_ref, weight_ref, real_ref, imag_ref, held, rows, part_sem, swap_sem, row_sem, send_sem):
+def whole_kernel(
+    table_ref, val_energy, cond_energy, sphere_ref, label_ref, psi_val, psi_cond, plane_ref, real_ref, imag_ref,
+    held, rows, val_all, cond_all, plane, val_rows, high, low, waves, picked, weight_ref, own_mask, got_mask,
+    load_sem, out_sem, in_sem, part_sem, swap_sem, row_sem, send_sem,
+):
     wide = lax.axis_index("wide")
     x = lax.axis_index("narrow")
     z, y, core = wide // 8, wide // 2 % 4, wide % 2
@@ -257,13 +287,40 @@
         "x+": (wide, (x + 1) % 4),
         "x-": (wide, (x + 3) % 4),
     }
+    def line(dz, dy):
+        return ((z + dz) % 4 * 8 + (y + dy) % 4 * 2 + core, x)
+
+    ring = [(wide, (x + d) % 4) for d in (1, 2, 3)]
+    twin = wide + 1 - 2 * core
+    near = ring + [(twin, x)] + [(twin, (x + d) % 4) for d in (1, 2, 3)]
+    far = [line(dz, dy) for dz in range(4) for dy in range(4) if dz or dy]
     barrier = pltpu.get_barrier_semaphore()
-    for peer in peers.values():
+    for peer in near + far:
         pl.semaphore_signal(barrier, inc=1, device_id=peer, device_id_type=MESH)
-
-    held[0, 0, 0:64, :] = own_ref[0:64, :]
-    held[0, 1, 0:64, :] = own_ref[64:128, :]
-    pl.semaphore_wait(barrier, len(peers))
+    loads = [
+        pltpu.make_async_copy(source, target, load_sem.at[i])
+        for i, (source, target) in enumerate(((psi_val, val_all), (psi_cond, cond_all), (plane_ref, plane)))
+    ]
+    for load in loads:
+        load.start()
+
+    band = lax.broadcasted_iota(jnp.int32, (128, 16), 0)
+    there = jnp.max(jnp.where(band == table_ref[0:1, :], 1, 0), axis=1, keepdims=True)
+    diagonal = lax.broadcasted_iota(jnp.int32, (128, 128), 0) == lax.broadcasted_iota(jnp.int32, (128, 128), 1)
+    mask = jnp.broadcast_to(jnp.max(jnp.where(diagonal, there, 0), axis=0, keepdims=True), (8, 128))
+    pl.semaphore_wait(barrier, len(near) + len(far))
+    present = exchange(mask, (near, far), own_mask, got_mask, out_sem, in_sem)
+    mine = deal(present, wide, val_energy[...], cond_energy[...], weight_ref)
+
+    for load in loads:
+        load.wait()
+    pick_rows(val_all, mine, val_rows)
+
+    def store(lane, width, real, imag):
+        held[0, 0, 0:64, pl.ds(lane, width)] = real
+        held[0, 1, 0:64, pl.ds(lane, width)] = imag
+
+    transform(val_rows, cond_all, plane, label_ref, sphere_ref, x * 2048, store, high, low, waves, picked)
 
     sends = []
 
@@ -382,7 +439,8 @@
         first = at(da, db)
         aa, bb = (b + da) % 4, (a + db) % 4
         second = jnp.where(core == 0, aa * 8 + bb * 2 + 1, bb * 8 + aa * 2)
-        return weight_ref[first] + weight_ref[second + 32]
+        lane = lax.broadcasted_iota(jnp.int32, (1, 256), 1)
+        return jnp.where(lane // 64 % 2 == 0, weight_ref[pl.ds(first, 1), :], weight_ref[pl.ds(second, 1), :])
 
     lag = 6
     for event in range(16 + lag):
@@ -415,52 +473,51 @@
                 row_copy(slot, which).wait_send()
 
 
-def gather_and_multiply(own, weights):
-    whole = pl.BlockSpec(memory_space=pltpu.VMEM)
+def on_device(psi_val, psi_cond, energy_val, energy_cond, pair_table, sphere_map):
+    vmem = pl.BlockSpec(memory_space=pltpu.VMEM)
+    hbm = pl.BlockSpec(memory_space=pl.ANY)
     return pl.pallas_call(
-        gather_kernel,
+        whole_kernel,
         out_shape=[jax.ShapeDtypeStruct((256, 2048), F32)] * 2,
-        in_specs=[whole] * 2,
-        out_specs=[whole] * 2,
+        in_specs=[vmem] * 5 + [hbm] * 3,
+        out_specs=[vmem] * 2,
         scratch_shapes=[
             pltpu.VMEM((16, 2, 128, 2048), BF),
             pltpu.VMEM((16, 2, 128, 256), BF),
+            pltpu.VMEM((128, FS**3), BF),
+            pltpu.VMEM((NC, FS**3), BF),
+            pltpu.VMEM((PLANE, 2 * HALF), BF),
+            pltpu.VMEM((8, FS**3), F32),
+            pltpu.VMEM((KX * 128, PLANE), BF),
+            pltpu.VMEM((KX * 128, PLANE), BF),
+            pltpu.VMEM((KX * 128, 2 * HALF), BF),
+            pltpu.VMEM((KX * 128, 256), F32),
+            pltpu.VMEM((32, 256), F32),
+            pltpu.VMEM((3, 8, 128), jnp.int32),
+            pltpu.VMEM((22, 8, 128), jnp.int32),
+            pltpu.SemaphoreType.DMA((3,)),
+            pltpu.SemaphoreType.DMA((22,)),
+            pltpu.SemaphoreType.DMA((22,)),
             pltpu.SemaphoreType.DMA((16, 2)),
             pltpu.SemaphoreType.DMA((16,)),
             pltpu.SemaphoreType.DMA((2, 16, 2)),
             pltpu.SemaphoreType.DMA((64,)),
         ],
         compiler_params=pltpu.CompilerParams(
-            collective_id=0, has_side_effects=True, vmem_limit_bytes=48 * 2**20
+            collective_id=0, has_side_effects=True, vmem_limit_bytes=58 * 2**20
         ),
-        cost_estimate=pl.CostEstimate(flops=2 * 4096 * 512 * 2048, bytes_accessed=8 * 2**20, transcendentals=0),
-        name="gather_and_multiply",
-    )(own, weights)
-
-
-def on_device(psi_val, psi_cond, energy_val, energy_cond, pair_table, sphere_map):
-    wide = lax.axis_index("wide")
-    bands = jnp.arange(128, dtype=jnp.int32)
-    present = jnp.max((pair_table[:, :1] == bands[None, :]).astype(F32), axis=0)
-    present = lax.psum(present, ("wide", "narrow")) > 0.5
-    rank = jnp.sum(((bands[:, None] < bands[None, :]) & present[:, None]).astype(jnp.int32), axis=0)
-    chosen = present[None, :] & (rank[None, :] == jnp.arange(VB, dtype=jnp.int32)[:, None])
-    band_of = jnp.sum(jnp.where(chosen, bands[None, :], 0), axis=1)
-    energy_of = jnp.sum(jnp.where(chosen, energy_val[None, :], 0.0), axis=1)
-    weight = 2.0 / ((energy_of[:, None] - energy_cond[None, :]) * math.sqrt(VB * NC))
-    weight = weight.reshape(32, 64)
-    blank = jnp.zeros_like(weight)
-    first = jnp.concatenate([weight, blank, weight, blank], axis=1)
-    second = jnp.concatenate([blank, weight, blank, weight], axis=1)
-    weights = jnp.concatenate([first, second], axis=0).reshape(64, 1, 256)
-    mine = lax.dynamic_slice(band_of, (2 * wide,), (2,))
-    val_rows = jnp.concatenate(
-        [lax.dynamic_slice(psi_val, (mine[i], 0), (1, psi_val.shape[1])) for i in range(2)], axis=0
-    ).astype(F32)
-    sphere_block = lax.dynamic_slice(sphere_map, (lax.axis_index("narrow") * 2048,), (2048,)).reshape(1, 2048)
-    own = transform(val_rows, psi_cond, sphere_block)
-    chi_real, chi_imag = gather_and_multiply(own, weights)
-    return (chi_real, chi_imag)
+        cost_estimate=pl.CostEstimate(flops=2 * 4096 * 512 * 2048, bytes_accessed=20 * 2**20, transcendentals=0),
+        name="polarizability",
+    )(
+        pair_table.T,
+        energy_val.reshape(1, -1),
+        energy_cond.reshape(1, -1),
+        sphere_map.reshape(1, -1),
+        jnp.asarray(plane_labels()),
+        psi_val,
+        psi_cond,
+        jnp.asarray(plane_table()).astype(BF),
+    )
 
 
 def solution(mesh):

time: 179 us -> 121 us (0.68)
  blocking collectives: 65.8 us -> 0 us
  Pallas kernels: 95.2 us -> 116 us
  local copies, waits for them, and re-layouts: 11 us -> 4.61 us
  between operations: 4.62 us -> 0.65 us
    psum x1 -> x0, blocking collectives: 65.8 us -> none  [on_device(): present = lax.psum(present, ('wide', 'narrow')) > 0.5]
    pallas_call x2 -> x1, Pallas kernels: 95.2 us -> 116 us  [on_device(): pl.pallas_call(whole_kernel, out_shape=[jax.ShapeDtypeStruct((256, 2048),...]
    dynamic_slice x3 -> x0, local copies, waits for them, and re-layouts: 2.26 us -> none  [the longest x1 1.49 us: on_device(): lax.dynamic_slice(psi_val, (mine[i], 0), (1, psi_val.shape[1]))]
    unnamed x8 -> x4, local copies, waits for them, and re-layouts: 6.4 us -> 4.61 us
where the time goes in v2:
time: 121 us
  Pallas kernels  116 us (96%)
  local copies, waits for them, and re-layouts  4.61 us (4%)
    pallas_call x1, Pallas kernels, on_device(): pl.pallas_call(whole_kernel, out_shape=[jax.ShapeDtypeStruct((256, 2048),...  116 us
    unnamed x4, local copies, waits for them, and re-layouts  4.61 us

profile of v2, /device:TPU:32, one launch (start us, length us, event | category | flops | bytes accessed | tf_op | source)
XLA Modules:
  0.0 121.3 jit_solution(14220779666118046095)
XLA Ops:
  0.6 116.1 %polarizability.1 = (f32[256,2048]{1,0:T(8,128)}, f32[256,2048]{1,0:T(8,128)}) custom-call(s32[2,16]{1,0:T(2,128)} %bitcast.5, f32[1,128]{1,0:T(1,128)} %bitcast.6, f32[1,32]{1,0:T(1,128)} %bitcast.7, s32[1,8192]{1,0:T(1,128)} %bitcast.4, s32[512,1]{1,0:T(8,128)} %constant.4.clone.label_ref, bf16[128,32768]{1,0:T(8,128)(2,1)} %psi_val.1, ...), custom_call_target="tpu_custom_call" | custom-call | flops 8589934592 | bytes 20971520 | tf_op jit(solution)/shard_map/polarizability/pallas_call | solution.py:479
  116.7 0.0 copy-start
  116.7 3.3 %copy.12 = f32[256,2048]{1,0:T(8,128)} copy(f32[256,2048]{1,0:T(8,128)} %get-tuple-element.4) | data formatting | bytes 4194304
  120.0 0.0 copy-done
  120.0 1.3 %copy.13 = f32[256,2048]{1,0:T(8,128)} copy(f32[256,2048]{1,0:T(8,128)S(1)} %copy-done) | data formatting | bytes 4194304
Async XLA Ops:
  116.7 3.3 %copy-start = (f32[256,2048]{1,0:T(8,128)S(1)}, f32[256,2048]{1,0:T(8,128)}, u32[]{:S(2)}) copy-start(f32[256,2048]{1,0:T(8,128)} %get-tuple-element.5) | copy-start | bytes 6291460

commit v3 on v2

v3 whole, which is shorter than its diff:
```python
import functools
import math

import jax
import jax.numpy as jnp
import numpy as np
from jax import lax
from jax.experimental import pallas as pl
from jax.experimental.pallas import tpu as pltpu
from jax.sharding import PartitionSpec as P

FS = 32
NC = 32
VB = 64
NG = 8192
PLANE = FS * FS
KX = 13
MESH = pl.DeviceIdType.MESH
BF = jnp.bfloat16
F32 = jnp.float32


def wrapped(index):
    return np.where(index >= FS // 2, index - FS, index)


def half_plane():
    index = np.arange(FS**3)
    length = wrapped(index // PLANE) ** 2 + wrapped(index // FS % FS) ** 2 + wrapped(index % FS) ** 2
    most = np.sort(length)[NG - 1]
    points = [
        (ky, kz)
        for ky in range(-15, 16)
        for kz in range(-15, 16)
        if ky * ky + kz * kz <= most and (ky > 0 or (ky == 0 and kz >= 0))
    ]
    points.sort(key=lambda point: (point[0] ** 2 + point[1] ** 2, point))
    return np.array(points)


POINTS = half_plane()
HALF = 256
TABLE_SCALE = 1.6211
TABLE_GAIN = 1.6245055860070914


NEAR = 128
FAR_KX = 9


def columns_of(first, second):
    return np.concatenate([first[:, :NEAR], second[:, :NEAR], first[:, NEAR:], second[:, NEAR:]], axis=1)


def plane_table():
    flat = np.arange(PLANE)
    phase = (flat // FS)[:, None] * POINTS[:, 0][None, :] + (flat % FS)[:, None] * POINTS[:, 1][None, :]
    angle = (phase % FS) * (2.0 * math.pi / FS)
    parts = []
    for wave in (np.cos(angle), np.sin(angle)):
        part = np.zeros((PLANE, HALF), np.float64)
        part[:, : len(POINTS)] = wave
        part[np.abs(part) < 1e-9] = 0.0
        parts.append(part)
    return (columns_of(*parts) * TABLE_SCALE).astype(np.float32)


def plane_labels():
    parts = np.full((2, HALF), -1, np.int32)
    for row, (ky, kz) in enumerate(POINTS):
        parts[0, row] = (ky % FS) * FS + kz % FS
        if (ky, kz) != (0, 0):
            parts[1, row] = (-ky % FS) * FS + (-kz) % FS
    return columns_of(parts[:1], parts[1:]).reshape(2 * HALF, 1)


def cosine(step):
    return math.cos(2.0 * math.pi * step / FS)


def combine(terms):
    total = None
    for factor, term in terms:
        if abs(factor) < 1e-12:
            continue
        if abs(abs(factor) - 1.0) < 1e-12:
            value = term
            if total is None:
                total = value if factor > 0 else -value
            else:
                total = total + value if factor > 0 else total - value
        else:
            value = term * factor
            total = value if total is None else total + value
    return total


def even_part(values, period, wanted):
    half = period // 2
    stride = FS // period
    out = {}
    odd = [k for k in wanted if k % 2]
    rest = [k for k in wanted if k % 2 == 0]
    if half == 1:
        for k in wanted:
            out[k] = values[0] + values[1] if k % 2 == 0 else values[0] - values[1]
        return out
    quarter = half // 2
    if odd:
        diff = [values[j] - values[half - j] for j in range(quarter)]
        for k in odd:
            out[k] = combine([(cosine(stride * j * k), diff[j]) for j in range(quarter)])
    if rest:
        folded = [values[j] + values[half - j] for j in range(quarter)] + [values[quarter]]
        inner = even_part(folded, half, [k // 2 for k in rest])
        for k in rest:
            out[k] = inner[k // 2]
    return out


def odd_part(values, period, wanted):
    half = period // 2
    stride = FS // period
    out = {}
    odd = [k for k in wanted if k % 2]
    rest = [k for k in wanted if k % 2 == 0]
    quarter = half // 2
    if odd:
        folded = [None] + [values[j] + values[half - j] for j in range(1, quarter)] + [values[quarter]]
        for k in odd:
            out[k] = combine(
                [(math.sin(2.0 * math.pi * stride * j * k / FS), folded[j]) for j in range(1, quarter + 1)]
            )
    if rest:
        live = [k for k in rest if k % half]
        if live:
            diff = [None] + [values[j] - values[half - j] for j in range(1, quarter)]
            inner = odd_part(diff, half, [k // 2 for k in live])
            for k in live:
                out[k] = inner[k // 2]
    return out


def exchange(mask, groups, own, got, out_sem, in_sem, work):
    own[0] = mask
    done, count = [], 0
    for step, group in enumerate(groups):
        copies = []
        for peer in group:
            copy = pltpu.make_async_remote_copy(
                src_ref=own.at[step],
                dst_ref=got.at[count],
                send_sem=out_sem.at[count],
                recv_sem=in_sem.at[count],
                device_id=peer,
                device_id_type=MESH,
            )
            copy.start()
            copies.append((copy, count))
            count += 1
        work(step)
        total = own[step]
        for copy, at in copies:
            copy.wait_recv()
            total = jnp.maximum(total, got[at])
        own[step + 1] = total
        done += copies
    for copy, _ in done:
        copy.wait_send()
    return own[len(groups)][0:1, :]


def deal(present, wide, val_energy, cond_energy, weight_ref):
    band = lax.broadcasted_iota(jnp.int32, (128, 128), 0)
    other = lax.broadcasted_iota(jnp.int32, (128, 128), 1)
    rank = jnp.sum(jnp.where(other < band, present, 0), axis=1, keepdims=True)
    across = jnp.sum(jnp.where(other == band, rank, 0), axis=0, keepdims=True)
    across = jnp.where(present > 0, across, -1)
    device = lax.broadcasted_iota(jnp.int32, (32, 128), 0)
    energy = [jnp.sum(jnp.where(across == 2 * device + i, val_energy, 0.0), axis=1, keepdims=True) for i in range(2)]
    lane = lax.broadcasted_iota(jnp.int32, (32, 256), 1)
    cond = jnp.concatenate([cond_energy] * 8, axis=1)
    gap = jnp.where(lane // NC % 2 == 0, energy[0], energy[1]) - cond
    weight_ref[...] = 2.0 / (gap * math.sqrt(VB * NC))
    row = lax.broadcasted_iota(jnp.int32, (8, 128), 0)
    return jnp.where((across == 2 * wide + row) & (row < 2), 1.0, 0.0)


def pick_rows(psi_ref, chosen, row_ref):
    blank = jnp.zeros_like(chosen[0:2])
    pad = jnp.zeros((4, 256), F32)
    both = jnp.concatenate([chosen[0:2], blank], axis=1)
    left = jnp.concatenate([both, jnp.concatenate([blank, chosen[0:2]], axis=1), pad], axis=0).astype(BF)
    half = PLANE // 2

    def step(x, carry):
        first = pl.ds(pl.multiple_of(x * PLANE, PLANE), half)
        second = pl.ds(pl.multiple_of(x * PLANE + half, half), half)
        right = jnp.concatenate([psi_ref[:, first], psi_ref[:, second]], axis=0)
        found = jnp.dot(left, right, preferred_element_type=F32)
        row_ref[0:2, first] = found[0:2]
        row_ref[0:2, second] = found[2:4]
        return carry

    lax.fori_loop(0, FS, step, 0)


WIDTH = 256


def columns_step(tile, label_ref, sphere_ref, first_column, hit, place):
    lane = pl.multiple_of(tile * WIDTH, WIDTH)
    flat = sphere_ref[:, pl.ds(pl.multiple_of(first_column + lane, WIDTH), WIDTH)]
    kx = flat // PLANE
    ky = flat // FS % FS
    kz = flat % FS
    mirror = kx >= FS // 2
    ky = jnp.where(mirror, (FS - ky) % FS, ky)
    kz = jnp.where(mirror, (FS - kz) % FS, kz)
    place[0:1, pl.ds(lane, WIDTH)] = jnp.where(mirror, FS - kx, kx)
    place[1:2, pl.ds(lane, WIDTH)] = jnp.where(mirror, -1, 1)
    target = ky * FS + kz
    hit[:, pl.ds(lane, WIDTH)] = jnp.where(label_ref[...] == target, 1.0, 0.0).astype(BF)


def transform_steps(first, count, val_ref, cond_ref, table_ref, hit, place, store, high, low, sums, waves, picked):
    lanes = 128
    rows = 16
    pair = 2 * count
    middle = FAR_KX * pair
    every = KX * pair

    def x_block(block):
        part, cond_row = (first + block * rows) // NC, (first + block * rows) % NC

        def x_step(step, carry):
            lane = pl.multiple_of(step * lanes, lanes)
            density = []
            for x in range(FS):
                at = pl.ds(pl.multiple_of(x * PLANE + lane, lanes), lanes)
                density.append(cond_ref[cond_row : cond_row + rows, at].astype(F32) * val_ref[part : part + 1, at])
            even = [density[0]] + [density[j] + density[FS - j] for j in range(1, 16)] + [density[16]]
            odd = [None] + [density[j] - density[FS - j] for j in range(1, 16)]
            real = even_part(even, FS, list(range(KX)))
            imag = odd_part(odd, FS, list(range(KX)))
            for k in range(KX):
                for s, value in ((0, real[k]), (1, imag.get(k))):
                    at = k * pair + s * count + block * rows
                    if value is None:
                        value = jnp.zeros((rows, lanes), F32)
                    if s == 1:
                        value = -value
                    top = value.astype(BF)
                    high[at : at + rows, pl.ds(lane, lanes)] = top
                    low[at : at + rows, pl.ds(lane, lanes)] = (value - top.astype(F32)).astype(BF)
            return carry

        lax.fori_loop(0, PLANE // lanes, x_step, 0)

    def plane(side):
        live = every if side == 0 else middle
        table = table_ref[:, side * HALF : (side + 1) * HALF]
        both = jnp.dot(high[0:live, :], table, preferred_element_type=F32)
        sums[0:live, :] = both + jnp.dot(low[0:live, :], table, preferred_element_type=F32)
        scale = FS ** (-1.5) / TABLE_GAIN
        left, right = side * HALF, side * HALF + NEAR

        def combine_step(k, carry):
            at = pl.multiple_of(k * pair, pair)
            re = pl.ds(at, count)
            im = pl.ds(pl.multiple_of(at + count, count), count)
            re_cos, re_sin = sums[re, :NEAR] * scale, sums[re, NEAR:] * scale
            im_cos, im_sin = sums[im, :NEAR] * scale, sums[im, NEAR:] * scale
            waves[re, left : left + NEAR] = (re_cos + im_sin).astype(BF)
            waves[re, right : right + NEAR] = (re_cos - im_sin).astype(BF)
            waves[im, left : left + NEAR] = (im_cos - re_sin).astype(BF)
            waves[im, right : right + NEAR] = (im_cos + re_sin).astype(BF)
            return carry

        lax.fori_loop(0, KX if side == 0 else FAR_KX, combine_step, 0)

    def pick(tiles):
        def pick_step(tile, carry):
            lane = pl.multiple_of(tile * WIDTH, WIDTH)
            at = pl.ds(lane, WIDTH)
            picked[0:middle, :] = jnp.dot(waves[0:middle, :], hit[:, at], preferred_element_type=F32)
            picked[middle:every, :] = jnp.dot(waves[middle:every, :HALF], hit[:HALF, at], preferred_element_type=F32)
            kx = place[0:1, at]
            total = picked[0:pair, :]
            for k in range(1, KX):
                total = jnp.where(kx == k, picked[k * pair : (k + 1) * pair, :], total)
            sign = place[1:2, at].astype(F32)
            store(lane, total[:count].astype(BF), (total[count:] * sign).astype(BF))
            return carry

        lax.fori_loop(tiles[0], tiles[1], pick_step, 0)

    steps = [functools.partial(x_block, block) for block in range(count // rows)]
    steps += [functools.partial(plane, side) for side in range(2)]
    tiles = 2048 // WIDTH
    return steps + [functools.partial(pick, (i, i + tiles // 4)) for i in range(0, tiles, tiles // 4)]


ORDER = [
    (0, 0), (3, 0), (1, 0), (0, 3), (0, 1), (2, 0), (3, 3), (3, 1),
    (1, 3), (1, 1), (0, 2), (2, 3), (2, 1), (3, 2), (1, 2), (2, 2),
]
SLOT = {place: slot for slot, place in enumerate(ORDER)}
COLORS = [(0, 64)]
SIZES = [last - first for first, last in COLORS]
MOST = max(SIZES)


def groups_of(size):
    count = max(1, 256 // (2 * size))
    return [(slot, min(slot + count, 16)) for slot in range(0, 16, count)]


def moves(slot):
    da, db = ORDER[slot]
    out = []
    if db == 0:
        if da == 0:
            out += [(None, "a+", SLOT[3, 0]), (None, "a-", SLOT[1, 0])]
        elif da == 3:
            out += [(0, "a+", SLOT[2, 0])]
        elif da == 1:
            out += [(1, "a-", SLOT[2, 0])]
        out += [(None, "b+", SLOT[da, 3]), (None, "b-", SLOT[da, 1])]
    elif db == 3:
        out += [(0, "b+", SLOT[da, 2])]
    elif db == 1:
        out += [(1, "b-", SLOT[da, 2])]
    return out


def in_halves(slot):
    da, db = ORDER[slot]
    return (da == 2 and db == 0) or db == 2


WAVES = [[0], [1, 2, 3, 4], [5, 6, 7], [8, 9, 10], [11, 12], [13, 14], [15]]
LATE = 11


def order_of_work():
    turns = [(color, wave) for wave in range(1, len(WAVES)) for color in range(len(COLORS))]
    turns = [(color, 0) for color in range(len(COLORS))] + turns
    order, left = [], {}
    for color, size in enumerate(SIZES):
        for group, (first, last) in enumerate(groups_of(size)):
            left[color, group] = set(range(first, last))
    for turn in range(len(turns) + 3):
        if turn < len(turns):
            color, wave = turns[turn]
            if wave == 0:
                order.append(("transform", color))
            order += [("own", slot, color) for slot in WAVES[wave]]
            order += [("swap", slot, color) for slot in WAVES[wave]]
        for back in range(4):
            if 0 <= turn - back < len(turns):
                color, wave = turns[turn - back]
                order.append(("rows", WAVES[wave], color, back))
        for back in range(4):
            if 0 <= turn - back < len(turns):
                color, wave = turns[turn - back]
                if back == (2 if WAVES[wave][0] >= LATE else 3):
                    for (of, group), slots in left.items():
                        if of == color and slots and slots <= set(WAVES[wave]):
                            order.append(("product", color, group))
                        if of == color:
                            slots -= set(WAVES[wave])
    return order


def whole_kernel(
    table_ref, val_energy, cond_energy, sphere_ref, label_ref, psi_val, psi_cond, plane_ref, real_ref, imag_ref,
    val_all, cond_all, plane, val_rows, hit, place, high, low, sums, waves, picked, weight_ref, own_mask, got_mask,
    load_sem, out_sem, in_sem, part_sem, swap_sem, row_sem, send_sem, *chunks,
):
    wide = lax.axis_index("wide")
    x = lax.axis_index("narrow")
    z, y, core = wide // 8, wide // 2 % 4, wide % 2
    a = jnp.where(core == 0, y, z)
    b = jnp.where(core == 0, z, y)

    def at(da, db, other=0):
        aa, bb = (a + da) % 4, (b + db) % 4
        return jnp.where(core == 0, bb * 8 + aa * 2, aa * 8 + bb * 2 + 1)

    peers = {
        "a+": (at(1, 0), x),
        "a-": (at(3, 0), x),
        "b+": (at(0, 1), x),
        "b-": (at(0, 3), x),
        "swap": (wide + 1 - 2 * core, x),
        "x+": (wide, (x + 1) % 4),
        "x-": (wide, (x + 3) % 4),
    }
    def line(dz, dy):
        return ((z + dz) % 4 * 8 + (y + dy) % 4 * 2 + core, x)

    ring = [(wide, (x + d) % 4) for d in (1, 2, 3)]
    twin = wide + 1 - 2 * core
    near = ring + [(twin, x)] + [(twin, (x + d) % 4) for d in (1, 2, 3)]
    far = [line(dz, dy) for dz in range(4) for dy in range(4) if dz or dy]
    barrier = pltpu.get_barrier_semaphore()
    for peer in near + far:
        pl.semaphore_signal(barrier, inc=1, device_id=peer, device_id_type=MESH)
    loads = [
        pltpu.make_async_copy(source, target, load_sem.at[i])
        for i, (source, target) in enumerate(((psi_val, val_all), (psi_cond, cond_all), (plane_ref, plane)))
    ]
    for load in loads:
        load.start()

    band = lax.broadcasted_iota(jnp.int32, (128, 16), 0)
    there = jnp.max(jnp.where(band == table_ref[0:1, :], 1, 0), axis=1, keepdims=True)
    diagonal = lax.broadcasted_iota(jnp.int32, (128, 128), 0) == lax.broadcasted_iota(jnp.int32, (128, 128), 1)
    mask = jnp.broadcast_to(jnp.max(jnp.where(diagonal, there, 0), axis=0, keepdims=True), (8, 128))
    pl.semaphore_wait(barrier, len(near) + len(far))

    def work(step):
        def columns(tile, carry):
            columns_step(tile, label_ref, sphere_ref, x * 2048, hit, place)
            return carry

        lax.fori_loop(step * 4, step * 4 + 4, columns, 0)

    present = exchange(mask, (near, far), own_mask, got_mask, out_sem, in_sem, work)
    mine = deal(present, wide, val_energy[...], cond_energy[...], weight_ref)

    for load in loads:
        load.wait()
    pick_rows(val_all, mine, val_rows)

    held, rows = chunks[: len(COLORS)], chunks[len(COLORS) :]

    def steps_of(color):
        first, last = COLORS[color]

        def store(lane, real, imag):
            held[color][0, 0, 0 : last - first, pl.ds(lane, WIDTH)] = real
            held[color][1, 0, 0 : last - first, pl.ds(lane, WIDTH)] = imag

        return transform_steps(
            first, last - first, val_rows, cond_all, plane, hit, place, store, high, low, sums, waves, picked
        )

    sends = []

    def view(slot, color, part, which=0):
        size = SIZES[color]
        if part is None:
            return held[color].at[:, slot, which * size : (which + 1) * size, :]
        return held[color].at[part, slot, which * size : (which + 1) * size, :]

    def part_copy(slot, color, part, peer, target, send):
        return pltpu.make_async_remote_copy(
            src_ref=view(slot, color, part),
            dst_ref=view(target, color, part),
            send_sem=send_sem.at[send],
            recv_sem=part_sem.at[target, color, part if part is not None else 0],
            device_id=peers[peer],
            device_id_type=MESH,
        )

    def swap_copy(slot, color, send):
        return pltpu.make_async_remote_copy(
            src_ref=view(slot, color, None, 0),
            dst_ref=view(slot, color, None, 1),
            send_sem=send_sem.at[send],
            recv_sem=swap_sem.at[slot, color],
            device_id=peers["swap"],
            device_id_type=MESH,
        )

    def own_event(slot, color):
        if slot and in_halves(slot):
            part_copy(slot, color, 0, "a+", slot, 0).wait_recv()
            part_copy(slot, color, 1, "a+", slot, 0).wait_recv()
        elif slot:
            part_copy(slot, color, None, "a+", slot, 0).wait_recv()
        copies = [part_copy(slot, color, part, way, target, len(sends) + i) for i, (part, way, target) in enumerate(moves(slot))]
        copies.append(swap_copy(slot, color, len(sends) + len(copies)))
        for copy in copies:
            copy.start()
        sends.extend(copies)

    column = pl.multiple_of((y * 2 + core) * 256, 256)
    hops = ((x - z) % 4, (z - x) % 4)

    def row_copy(slot, color, which, way):
        size = SIZES[color]
        ref = rows[color].at[:, slot, which * size : (which + 1) * size, :]
        return pltpu.make_async_remote_copy(
            src_ref=ref,
            dst_ref=ref,
            send_sem=row_sem.at[1 + way, slot, color, which],
            recv_sem=row_sem.at[0, slot, color, which],
            device_id=peers["x+" if way == 0 else "x-"],
            device_id_type=MESH,
        )

    def row_ways(slot, which, hop):
        if slot < LATE:
            return [which] if hop < 3 else []
        return [0, 1] if hop == 0 else [which] if hop == 1 else []

    def row_events(slots, color, step):
        late = slots[0] >= LATE
        for which in range(2):
            for hop in ([step] if not late else [0] if step == 0 else [1, 3] if step == 1 else [2] if step == 2 else []):

                @pl.when(hops[which] == hop)
                def _():
                    at = slice(which * SIZES[color], (which + 1) * SIZES[color])
                    for slot in slots:
                        if hop == 0:
                            rows[color][:, slot, at, :] = held[color][:, slot, at, pl.ds(column, 256)]
                        else:
                            row_copy(slot, color, which, 0).wait_recv()
                        for way in row_ways(slot, which, hop):
                            row_copy(slot, color, which, way).start()

    width = 512

    def product(color, group, start):
        first, last = groups_of(SIZES[color])[group]
        depth = (last - first) * 2 * SIZES[color]
        weight = jnp.concatenate([weight_of(slot, color, which) for slot in range(first, last) for which in range(2)], axis=1)
        left = [(rows[color][part, first:last].reshape(depth, 256).astype(F32).T * weight).astype(BF) for part in range(2)]
        left_real = jnp.concatenate([left[0], left[1]], axis=0)
        left_imag = jnp.concatenate([left[1], -left[0]], axis=0)

        def tile(step, carry):
            at = pl.ds(pl.multiple_of(step * width, width), width)
            right = [held[color][part, first:last, :, at].reshape(depth, width) for part in range(2)]
            both = jnp.dot(left_real, right[0], preferred_element_type=F32)
            both = both + jnp.dot(left_imag, right[1], preferred_element_type=F32)
            return at, both

        def first_tile(step, carry):
            at, both = tile(step, carry)
            real_ref[:, at] = both[:256]
            imag_ref[:, at] = both[256:]
            return carry

        def later_tile(step, carry):
            at, both = tile(step, carry)
            real_ref[:, at] += both[:256]
            imag_ref[:, at] += both[256:]
            return carry

        lax.fori_loop(0, 2048 // width, first_tile if start else later_tile, 0)

    def weight_of(slot, color, which):
        da, db = ORDER[slot]
        device = at(da, db)
        if which:
            aa, bb = (b + da) % 4, (a + db) % 4
            device = jnp.where(core == 0, aa * 8 + bb * 2 + 1, bb * 8 + aa * 2)
        return weight_ref[pl.ds(device, 1), :][:, COLORS[color][0] : COLORS[color][1]]

    start = True
    for kind, *place_of in order_of_work():
        if kind == "transform":
            for step in steps_of(*place_of):
                step()
        elif kind == "own":
            own_event(*place_of)
        elif kind == "swap":
            swap_copy(*place_of, 0).wait_recv()
        elif kind == "rows":
            row_events(*place_of)
        else:
            product(*place_of, start)
            start = False

    for copy in sends:
        copy.wait_send()
    for which in range(2):
        for hop in range(3):

            @pl.when(hops[which] == hop)
            def _():
                for slot in range(16):
                    for color in range(len(COLORS)):
                        for way in row_ways(slot, which, hop):
                            row_copy(slot, color, which, way).wait_send()


def on_device(psi_val, psi_cond, energy_val, energy_cond, pair_table, sphere_map):
    vmem = pl.BlockSpec(memory_space=pltpu.VMEM)
    hbm = pl.BlockSpec(memory_space=pl.ANY)
    return pl.pallas_call(
        whole_kernel,
        out_shape=[jax.ShapeDtypeStruct((256, 2048), F32)] * 2,
        in_specs=[vmem] * 5 + [hbm] * 3,
        out_specs=[vmem] * 2,
        scratch_shapes=[
            pltpu.VMEM((128, FS**3), BF),
            pltpu.VMEM((NC, FS**3), BF),
            pltpu.VMEM((PLANE, 2 * HALF), BF),
            pltpu.VMEM((8, FS**3), F32),
            pltpu.VMEM((2 * HALF, 2048), BF),
            pltpu.VMEM((2, 2048), jnp.int32),
            pltpu.VMEM((KX * 2 * MOST, PLANE), BF),
            pltpu.VMEM((KX * 2 * MOST, PLANE), BF),
            pltpu.VMEM((KX * 2 * MOST, HALF), F32),
            pltpu.VMEM((KX * 2 * MOST, 2 * HALF), BF),
            pltpu.VMEM((KX * 2 * MOST, WIDTH), F32),
            pltpu.VMEM((32, 256), F32),
            pltpu.VMEM((3, 8, 128), jnp.int32),
            pltpu.VMEM((22, 8, 128), jnp.int32),
            pltpu.SemaphoreType.DMA((3,)),
            pltpu.SemaphoreType.DMA((22,)),
            pltpu.SemaphoreType.DMA((22,)),
            pltpu.SemaphoreType.DMA((16, len(COLORS), 2)),
            pltpu.SemaphoreType.DMA((16, len(COLORS))),
            pltpu.SemaphoreType.DMA((3, 16, len(COLORS), 2)),
            pltpu.SemaphoreType.DMA((48 * len(COLORS),)),
        ]
        + [pltpu.VMEM((2, 16, 2 * size, 2048), BF) for size in SIZES]
        + [pltpu.VMEM((2, 16, 2 * size, 256), BF) for size in SIZES],
        compiler_params=pltpu.CompilerParams(
            collective_id=0, has_side_effects=True, vmem_limit_bytes=58 * 2**20
        ),
        cost_estimate=pl.CostEstimate(flops=2 * 4096 * 512 * 2048, bytes_accessed=20 * 2**20, transcendentals=0),
        name="polarizability",
    )(
        pair_table.T,
        energy_val.reshape(1, -1),
        energy_cond.reshape(1, -1),
        sphere_map.reshape(1, -1),
        jnp.asarray(plane_labels()),
        psi_val,
        psi_cond,
        jnp.asarray(plane_table()).astype(BF),
    )


def solution(mesh):
    placed = (P(), P(), P(), P(), P(("wide", "narrow"), None), P())
    return jax.shard_map(
        on_device,
        mesh=mesh,
        in_specs=placed,
        out_specs=(P("wide", "narrow"), P("wide", "narrow")),
        check_vma=False,
    )
```

time: 121 us -> 110 us (0.909)
  the two profiles are of different devices: /device:TPU:32 before, /device:TPU:4 now
where the time goes in v3:
time: 110 us
  Pallas kernels  105 us (95%)
  local copies, waits for them, and re-layouts  4.61 us (4%)
    pallas_call x1, Pallas kernels, on_device(): pl.pallas_call(whole_kernel, out_shape=[jax.ShapeDtypeStruct((256, 2048),...  105 us
    unnamed x4, local copies, waits for them, and re-layouts  4.61 us

profile of v3, /device:TPU:4, one launch (start us, length us, event | category | flops | bytes accessed | tf_op | source)
XLA Modules:
  0.0 109.8 jit_solution(17803573223454735218)
XLA Ops:
  0.6 104.5 %polarizability.1 = (f32[256,2048]{1,0:T(8,128)}, f32[256,2048]{1,0:T(8,128)}) custom-call(s32[2,16]{1,0:T(2,128)} %bitcast.5, f32[1,128]{1,0:T(1,128)} %bitcast.6, f32[1,32]{1,0:T(1,128)} %bitcast.7, s32[1,8192]{1,0:T(1,128)} %bitcast.4, s32[512,1]{1,0:T(8,128)} %constant.4.clone.label_ref, bf16[128,32768]{1,0:T(8,128)(2,1)} %psi_val.1, ...), custom_call_target="tpu_custom_call" | custom-call | flops 8589934592 | bytes 20971520 | tf_op jit(solution)/shard_map/polarizability/pallas_call | solution.py:596
  105.2 0.0 copy-start
  105.2 3.3 %copy.12 = f32[256,2048]{1,0:T(8,128)} copy(f32[256,2048]{1,0:T(8,128)} %get-tuple-element.4) | data formatting | bytes 4194304
  108.5 0.0 copy-done
  108.5 1.3 %copy.13 = f32[256,2048]{1,0:T(8,128)} copy(f32[256,2048]{1,0:T(8,128)S(1)} %copy-done) | data formatting | bytes 4194304
Async XLA Ops:
  105.2 3.3 %copy-start = (f32[256,2048]{1,0:T(8,128)S(1)}, f32[256,2048]{1,0:T(8,128)}, u32[]{:S(2)}) copy-start(f32[256,2048]{1,0:T(8,128)} %get-tuple-element.5) | copy-start | bytes 6291460

commit v4 on v3

--- a/solution.py
+++ b/solution.py
@@ -187,19 +187,11 @@
 
 
 def pick_rows(psi_ref, chosen, row_ref):
-    blank = jnp.zeros_like(chosen[0:2])
-    pad = jnp.zeros((4, 256), F32)
-    both = jnp.concatenate([chosen[0:2], blank], axis=1)
-    left = jnp.concatenate([both, jnp.concatenate([blank, chosen[0:2]], axis=1), pad], axis=0).astype(BF)
-    half = PLANE // 2
+    left = chosen.astype(BF)
 
     def step(x, carry):
-        first = pl.ds(pl.multiple_of(x * PLANE, PLANE), half)
-        second = pl.ds(pl.multiple_of(x * PLANE + half, half), half)
-        right = jnp.concatenate([psi_ref[:, first], psi_ref[:, second]], axis=0)
-        found = jnp.dot(left, right, preferred_element_type=F32)
-        row_ref[0:2, first] = found[0:2]
-        row_ref[0:2, second] = found[2:4]
+        at = pl.ds(pl.multiple_of(x * PLANE, PLANE), PLANE)
+        row_ref[:, at] = jnp.dot(left, psi_ref[:, at], preferred_element_type=F32)
         return carry
 
     lax.fori_loop(0, FS, step, 0)
@@ -306,13 +298,14 @@
     (1, 3), (1, 1), (0, 2), (2, 3), (2, 1), (3, 2), (1, 2), (2, 2),
 ]
 SLOT = {place: slot for slot, place in enumerate(ORDER)}
-COLORS = [(0, 64)]
+COLORS = [(0, 32), (32, 64)]
 SIZES = [last - first for first, last in COLORS]
 MOST = max(SIZES)
+DEPTH = 512
 
 
 def groups_of(size):
-    count = max(1, 256 // (2 * size))
+    count = max(1, DEPTH // (2 * size))
     return [(slot, min(slot + count, 16)) for slot in range(0, 16, count)]
 
 
@@ -349,27 +342,33 @@
     order, left = [], {}
     for color, size in enumerate(SIZES):
         for group, (first, last) in enumerate(groups_of(size)):
-            left[color, group] = set(range(first, last))
-    for turn in range(len(turns) + 3):
+            left[color, group] = {(slot, which) for slot in range(first, last) for which in range(2)}
+    for turn in range(len(turns) + 5):
         if turn < len(turns):
             color, wave = turns[turn]
             if wave == 0:
                 order.append(("transform", color))
-            order += [("own", slot, color) for slot in WAVES[wave]]
-            order += [("swap", slot, color) for slot in WAVES[wave]]
-        for back in range(4):
-            if 0 <= turn - back < len(turns):
-                color, wave = turns[turn - back]
-                order.append(("rows", WAVES[wave], color, back))
-        for back in range(4):
-            if 0 <= turn - back < len(turns):
-                color, wave = turns[turn - back]
-                if back == (2 if WAVES[wave][0] >= LATE else 3):
-                    for (of, group), slots in left.items():
-                        if of == color and slots and slots <= set(WAVES[wave]):
-                            order.append(("product", color, group))
-                        if of == color:
-                            slots -= set(WAVES[wave])
+            order += [("arrive", slot, color) for slot in WAVES[wave]]
+        ripe = []
+        for step in range(4):
+            for before, (color, wave) in enumerate(turns):
+                for which in range(2):
+                    lag = step + (which if wave + 1 < len(WAVES) else 0)
+                    if before + lag == turn:
+                        if which and step == 0:
+                            order += [("swap", slot, color) for slot in WAVES[wave]]
+                        order.append(("rows", wave, color, which, step))
+                        if step == (2 if WAVES[wave][0] >= LATE else 3):
+                            ripe += [(color, slot, which) for slot in WAVES[wave]]
+        if turn < len(turns):
+            color, wave = turns[turn]
+            order += [("push", slot, color) for slot in WAVES[wave]]
+        for color, slot, which in ripe:
+            for (of, group), slices in left.items():
+                if of == color and (slot, which) in slices:
+                    slices.remove((slot, which))
+                    if not slices:
+                        order.append(("product", color, group))
     return order
 
 
@@ -475,53 +474,57 @@
             device_id_type=MESH,
         )
 
-    def own_event(slot, color):
+    def arrive_event(slot, color):
         if slot and in_halves(slot):
             part_copy(slot, color, 0, "a+", slot, 0).wait_recv()
             part_copy(slot, color, 1, "a+", slot, 0).wait_recv()
         elif slot:
             part_copy(slot, color, None, "a+", slot, 0).wait_recv()
-        copies = [part_copy(slot, color, part, way, target, len(sends) + i) for i, (part, way, target) in enumerate(moves(slot))]
-        copies.append(swap_copy(slot, color, len(sends) + len(copies)))
-        for copy in copies:
+        copy = swap_copy(slot, color, len(sends))
+        copy.start()
+        sends.append(copy)
+
+    def push_event(slot, color):
+        for part, way, target in moves(slot):
+            copy = part_copy(slot, color, part, way, target, len(sends))
             copy.start()
-        sends.extend(copies)
+            sends.append(copy)
 
     column = pl.multiple_of((y * 2 + core) * 256, 256)
     hops = ((x - z) % 4, (z - x) % 4)
 
-    def row_copy(slot, color, which, way):
+    def row_copy(wave, color, which, way):
         size = SIZES[color]
-        ref = rows[color].at[:, slot, which * size : (which + 1) * size, :]
+        slots = WAVES[wave]
+        ref = rows[color].at[:, slots[0] : slots[-1] + 1, which * size : (which + 1) * size, :]
         return pltpu.make_async_remote_copy(
             src_ref=ref,
             dst_ref=ref,
-            send_sem=row_sem.at[1 + way, slot, color, which],
-            recv_sem=row_sem.at[0, slot, color, which],
+            send_sem=row_sem.at[1 + way, wave, color, which],
+            recv_sem=row_sem.at[0, wave, color, which],
             device_id=peers["x+" if way == 0 else "x-"],
             device_id_type=MESH,
         )
 
-    def row_ways(slot, which, hop):
-        if slot < LATE:
+    def row_ways(wave, which, hop):
+        if WAVES[wave][0] < LATE:
             return [which] if hop < 3 else []
         return [0, 1] if hop == 0 else [which] if hop == 1 else []
 
-    def row_events(slots, color, step):
-        late = slots[0] >= LATE
-        for which in range(2):
-            for hop in ([step] if not late else [0] if step == 0 else [1, 3] if step == 1 else [2] if step == 2 else []):
-
-                @pl.when(hops[which] == hop)
-                def _():
+    def row_events(wave, color, which, step):
+        late = WAVES[wave][0] >= LATE
+        for hop in [step] if not late else [0] if step == 0 else [1, 3] if step == 1 else [2] if step == 2 else []:
+
+            @pl.when(hops[which] == hop)
+            def _():
+                if hop == 0:
                     at = slice(which * SIZES[color], (which + 1) * SIZES[color])
-                    for slot in slots:
-                        if hop == 0:
-                            rows[color][:, slot, at, :] = held[color][:, slot, at, pl.ds(column, 256)]
-                        else:
-                            row_copy(slot, color, which, 0).wait_recv()
-                        for way in row_ways(slot, which, hop):
-                            row_copy(slot, color, which, way).start()
+                    for slot in WAVES[wave]:
+                        rows[color][:, slot, at, :] = held[color][:, slot, at, pl.ds(column, 256)]
+                else:
+                    row_copy(wave, color, which, 0).wait_recv()
+                for way in row_ways(wave, which, hop):
+                    row_copy(wave, color, which, way).start()
 
     width = 512
 
@@ -567,8 +570,10 @@
         if kind == "transform":
             for step in steps_of(*place_of):
                 step()
-        elif kind == "own":
-            own_event(*place_of)
+        elif kind == "arrive":
+            arrive_event(*place_of)
+        elif kind == "push":
+            push_event(*place_of)
         elif kind == "swap":
             swap_copy(*place_of, 0).wait_recv()
         elif kind == "rows":
@@ -584,10 +589,10 @@
 
             @pl.when(hops[which] == hop)
             def _():
-                for slot in range(16):
+                for wave in range(len(WAVES)):
                     for color in range(len(COLORS)):
-                        for way in row_ways(slot, which, hop):
-                            row_copy(slot, color, which, way).wait_send()
+                        for way in row_ways(wave, which, hop):
+                            row_copy(wave, color, which, way).wait_send()
 
 
 def on_device(psi_val, psi_cond, energy_val, energy_cond, pair_table, sphere_map):
@@ -618,7 +623,7 @@
             pltpu.SemaphoreType.DMA((22,)),
             pltpu.SemaphoreType.DMA((16, len(COLORS), 2)),
             pltpu.SemaphoreType.DMA((16, len(COLORS))),
-            pltpu.SemaphoreType.DMA((3, 16, len(COLORS), 2)),
+            pltpu.SemaphoreType.DMA((3, len(WAVES), len(COLORS), 2)),
             pltpu.SemaphoreType.DMA((48 * len(COLORS),)),
         ]
         + [pltpu.VMEM((2, 16, 2 * size, 2048), BF) for size in SIZES]

time: 110 us -> 105 us (0.955)
  Pallas kernels: 105 us -> 99.5 us
    pallas_call x1, Pallas kernels: 105 us -> 99.5 us  [on_device(): pl.pallas_call(whole_kernel, out_shape=[jax.ShapeDtypeStruct((256, 2048),...]
where the time goes in v4:
time: 105 us
  Pallas kernels  99.5 us (95%)
  local copies, waits for them, and re-layouts  4.61 us (4%)
    pallas_call x1, Pallas kernels, on_device(): pl.pallas_call(whole_kernel, out_shape=[jax.ShapeDtypeStruct((256, 2048),...  99.5 us
    unnamed x4, local copies, waits for them, and re-layouts  4.61 us

profile of v4, /device:TPU:4, one launch (start us, length us, event | category | flops | bytes accessed | tf_op | source)
XLA Modules:
  0.0 104.7 jit_solution(1898013488048085027)
XLA Ops:
  0.6 99.5 %polarizability.1 = (f32[256,2048]{1,0:T(8,128)}, f32[256,2048]{1,0:T(8,128)}) custom-call(s32[2,16]{1,0:T(2,128)} %bitcast.5, f32[1,128]{1,0:T(1,128)} %bitcast.6, f32[1,32]{1,0:T(1,128)} %bitcast.7, s32[1,8192]{1,0:T(1,128)} %bitcast.4, s32[512,1]{1,0:T(8,128)} %constant.4.clone.label_ref, bf16[128,32768]{1,0:T(8,128)(2,1)} %psi_val.1, ...), custom_call_target="tpu_custom_call" | custom-call | flops 8589934592 | bytes 20971520 | tf_op jit(solution)/shard_map/polarizability/pallas_call | solution.py:601
  100.1 0.0 copy-start
  100.1 3.3 %copy.12 = f32[256,2048]{1,0:T(8,128)} copy(f32[256,2048]{1,0:T(8,128)} %get-tuple-element.4) | data formatting | bytes 4194304
  103.4 0.0 copy-done
  103.4 1.3 %copy.13 = f32[256,2048]{1,0:T(8,128)} copy(f32[256,2048]{1,0:T(8,128)S(1)} %copy-done) | data formatting | bytes 4194304
Async XLA Ops:
  100.1 3.3 %copy-start = (f32[256,2048]{1,0:T(8,128)S(1)}, f32[256,2048]{1,0:T(8,128)}, u32[]{:S(2)}) copy-start(f32[256,2048]{1,0:T(8,128)} %get-tuple-element.5) | copy-start | bytes 6291460

commit v5 on v4

--- a/solution.py
+++ b/solution.py
@@ -186,17 +186,6 @@
     return jnp.where((across == 2 * wide + row) & (row < 2), 1.0, 0.0)
 
 
-def pick_rows(psi_ref, chosen, row_ref):
-    left = chosen.astype(BF)
-
-    def step(x, carry):
-        at = pl.ds(pl.multiple_of(x * PLANE, PLANE), PLANE)
-        row_ref[:, at] = jnp.dot(left, psi_ref[:, at], preferred_element_type=F32)
-        return carry
-
-    lax.fori_loop(0, FS, step, 0)
-
-
 WIDTH = 256
 
 
@@ -215,18 +204,24 @@
     hit[:, pl.ds(lane, WIDTH)] = jnp.where(label_ref[...] == target, 1.0, 0.0).astype(BF)
 
 
-def transform_steps(first, count, val_ref, cond_ref, table_ref, hit, place, store, high, low, sums, waves, picked):
+def transform_steps(first, count, chosen, psi_ref, val_ref, cond_ref, table_ref, hit, place, store, high, low, sums, waves, picked):
     lanes = 128
     rows = 16
     pair = 2 * count
     middle = FAR_KX * pair
     every = KX * pair
 
-    def x_block(block):
-        part, cond_row = (first + block * rows) // NC, (first + block * rows) % NC
-
-        def x_step(step, carry):
-            lane = pl.multiple_of(step * lanes, lanes)
+    def rows_at(step):
+        for x in range(FS):
+            at = pl.ds(pl.multiple_of(x * PLANE + step * lanes, lanes), lanes)
+            val_ref[:, at] = jnp.dot(chosen.astype(BF), psi_ref[:, at], preferred_element_type=F32)
+
+    def x_step(step, carry):
+        lane = pl.multiple_of(step * lanes, lanes)
+        if chosen is not None:
+            rows_at(step)
+        for block in range(count // rows):
+            part, cond_row = (first + block * rows) // NC, (first + block * rows) % NC
             density = []
             for x in range(FS):
                 at = pl.ds(pl.multiple_of(x * PLANE + lane, lanes), lanes)
@@ -245,8 +240,9 @@
                     top = value.astype(BF)
                     high[at : at + rows, pl.ds(lane, lanes)] = top
                     low[at : at + rows, pl.ds(lane, lanes)] = (value - top.astype(F32)).astype(BF)
-            return carry
-
+        return carry
+
+    def x_all():
         lax.fori_loop(0, PLANE // lanes, x_step, 0)
 
     def plane(side):
@@ -287,8 +283,7 @@
 
         lax.fori_loop(tiles[0], tiles[1], pick_step, 0)
 
-    steps = [functools.partial(x_block, block) for block in range(count // rows)]
-    steps += [functools.partial(plane, side) for side in range(2)]
+    steps = [x_all] + [functools.partial(plane, side) for side in range(2)]
     tiles = 2048 // WIDTH
     return steps + [functools.partial(pick, (i, i + tiles // 4)) for i in range(0, tiles, tiles // 4)]
 
@@ -431,7 +426,6 @@
 
     for load in loads:
         load.wait()
-    pick_rows(val_all, mine, val_rows)
 
     held, rows = chunks[: len(COLORS)], chunks[len(COLORS) :]
 
@@ -443,7 +437,7 @@
             held[color][1, 0, 0 : last - first, pl.ds(lane, WIDTH)] = imag
 
         return transform_steps(
-            first, last - first, val_rows, cond_all, plane, hit, place, store, high, low, sums, waves, picked
+            first, last - first, mine if color == 0 else None, val_all, val_rows, cond_all, plane, hit, place, store, high, low, sums, waves, picked
         )
 
     sends = []

time: 105 us -> 103 us (0.981)
  Pallas kernels: 99.5 us -> 97.9 us
    pallas_call x1, Pallas kernels: 99.5 us -> 97.9 us  [on_device(): pl.pallas_call(whole_kernel, out_shape=[jax.ShapeDtypeStruct((256, 2048),...]
where the time goes in v5:
time: 103 us
  Pallas kernels  97.9 us (95%)
  local copies, waits for them, and re-layouts  4.61 us (4%)
    pallas_call x1, Pallas kernels, on_device(): pl.pallas_call(whole_kernel, out_shape=[jax.ShapeDtypeStruct((256, 2048),...  97.9 us
    unnamed x4, local copies, waits for them, and re-layouts  4.61 us

profile of v5, /device:TPU:4, one launch (start us, length us, event | category | flops | bytes accessed | tf_op | source)
XLA Modules:
  0.0 103.1 jit_solution(13346835713324433156)
XLA Ops:
  0.6 97.9 %polarizability.1 = (f32[256,2048]{1,0:T(8,128)}, f32[256,2048]{1,0:T(8,128)}) custom-call(s32[2,16]{1,0:T(2,128)} %bitcast.5, f32[1,128]{1,0:T(1,128)} %bitcast.6, f32[1,32]{1,0:T(1,128)} %bitcast.7, s32[1,8192]{1,0:T(1,128)} %bitcast.4, s32[512,1]{1,0:T(8,128)} %constant.4.clone.label_ref, bf16[128,32768]{1,0:T(8,128)(2,1)} %psi_val.1, ...), custom_call_target="tpu_custom_call" | custom-call | flops 8589934592 | bytes 20971520 | tf_op jit(solution)/shard_map/polarizability/pallas_call | solution.py:595
  98.5 0.0 copy-start
  98.5 3.3 %copy.12 = f32[256,2048]{1,0:T(8,128)} copy(f32[256,2048]{1,0:T(8,128)} %get-tuple-element.4) | data formatting | bytes 4194304
  101.8 0.0 copy-done
  101.8 1.3 %copy.13 = f32[256,2048]{1,0:T(8,128)} copy(f32[256,2048]{1,0:T(8,128)S(1)} %copy-done) | data formatting | bytes 4194304
Async XLA Ops:
  98.5 3.3 %copy-start = (f32[256,2048]{1,0:T(8,128)S(1)}, f32[256,2048]{1,0:T(8,128)}, u32[]{:S(2)}) copy-start(f32[256,2048]{1,0:T(8,128)} %get-tuple-element.5) | copy-start | bytes 6291460
